TPU v7x, 32 devices: a whole 2x2x4 slice. The times are simulated.
32 devices in a mesh: gx: 8 (over y, x, core), gy: 4 (over z).
Axes of the slice: x: 2, y: 2, z: 4, core: 2. Of those that a mesh axis runs over, the one named last changes fastest.
Arguments:
- pressure: float32 [10, 512, 512], P(None, 'gx', 'gy'), may hold values from -6 to 6
- sat_old: float32 [10, 512, 512], P(None, 'gx', 'gy'), may hold values from 0.3 to 1
- soil_type: int32 [10, 512, 512], P(None, 'gx', 'gy'), may hold values from 0 to 12
- ks_table: float32 [13], replicated, may hold values from 0.1 to 2
- alpha_table: float32 [13], replicated, may hold values from 0.5 to 4
- porosity_table: float32 [13], replicated, may hold values from 0.2 to 0.5
- rain: float32 [262144], P(('gx', 'gy')), may hold values from 0 to 2
- evapo: float32 [262144], P(('gx', 'gy')), may hold values from 0 to 1
- land_mask: int32 [262144], P(('gx', 'gy')), may hold values 0 or 1
- tile: int32 [262144, 1], P(('gx', 'gy')), may hold values from 0 to 31; in each aligned block of 8192 rows (0 to 8191, 8192 to 16383, ...) at most 256 rows name the same one
- cell: int32 [262144], P(('gx', 'gy')), may hold values from 0 to 8191
- theta: float32 [10, 262144], P(None, ('gx', 'gy')), may hold values from 0.1 to 0.5
- kappa: float32 [10, 262144], P(None, ('gx', 'gy')), may hold values from 0.2 to 5
Outputs:
- pressure_next: float32 [10, 512, 512], P(None, 'gx', 'gy')
- residual_next: float32 [10, 512, 512], P(None, 'gx', 'gy')
- theta_next: float32 [10, 262144], P(None, ('gx', 'gy'))
Inputs may be any that keep to these rules, and one draw needn't show every extreme that they name: Among the 8192 land columns of one device at most 256 name the same tile, and that many do in some device.
All inputs are finite; a program needn't handle non-finite values. No bound on the sum of `land_mask` on one device may be relied on, other than what follows from the above.
Results may differ from a plain program's by a relative error of at most 0.0003.
Values sent between devices are 32-bit elements; how exact they have to be, the bound alone decides.
A program may use at most 128 MiB of HBM per device.

v0:
```python
import jax
import jax.numpy as jnp
from jax import lax
from jax.sharding import PartitionSpec as P


def padded(block, sides, width):
    for axis, dim in sides:
        count = lax.axis_size(axis)
        forward = [(i, i + 1) for i in range(count - 1)]
        backward = [(target, source) for source, target in forward]
        low = lax.ppermute(
            lax.slice_in_dim(block, block.shape[dim] - width, None, axis=dim), axis, forward
        )
        high = lax.ppermute(lax.slice_in_dim(block, 0, width, axis=dim), axis, backward)
        block = jnp.concatenate([low, block, high], axis=dim)
    return block


def relperm(p, alpha):
    head = alpha * jnp.maximum(-p, 0.0)
    return 1.0 / (1.0 + head * head)


def mean_face(first, second):
    total = first + second
    return jnp.where(
        first * second > 0, 2.0 * first * second / jnp.where(total > 0, total, 1.0), 0.0
    )


def residual_core(padp, padk, pada, sat_old, phi, source):
    width_a = padp.shape[1] - 2
    width_b = padp.shape[2] - 2
    krel = relperm(padp, pada)
    p_mid = padp[:, 1:-1, 1:-1]
    k_mid = padk[:, 1:-1, 1:-1]
    r_mid = krel[:, 1:-1, 1:-1]
    outflow = jnp.zeros_like(p_mid)
    for sx, sy in ((0, 1), (2, 1), (1, 0), (1, 2)):
        p_nb = padp[:, sx : sx + width_a, sy : sy + width_b]
        k_nb = padk[:, sx : sx + width_a, sy : sy + width_b]
        r_nb = krel[:, sx : sx + width_a, sy : sy + width_b]
        outflow = outflow + mean_face(k_mid, k_nb) * 0.5 * (r_mid + r_nb) * (p_mid - p_nb)
    down = (
        mean_face(k_mid[:-1], k_mid[1:])
        * 0.5
        * (r_mid[:-1] + r_mid[1:])
        * (p_mid[:-1] - p_mid[1:] + 1.0)
    )
    outflow = (
        outflow + jnp.pad(down, ((0, 1), (0, 0), (0, 0))) - jnp.pad(down, ((1, 0), (0, 0), (0, 0)))
    )
    return phi * (jnp.sqrt(r_mid) - sat_old) + 0.5 * outflow - 0.5 * source


def soil_solve(theta, kappa, p_top, s_top):
    levels = theta.shape[0]
    coeff = kappa * (0.5 + s_top)[None, :]
    upper_list = []
    value_list = []
    for level in range(levels):
        below = coeff[level + 1] if level + 1 < levels else jnp.zeros_like(coeff[0])
        diag = 1.0 + coeff[level] + below
        rhs = theta[level] + coeff[0] * p_top if level == 0 else theta[level]
        if level == 0:
            denom = diag
            value = rhs / denom
        else:
            denom = diag + coeff[level] * upper_list[-1]
            value = (rhs + coeff[level] * value_list[-1]) / denom
        upper_list.append(-below / denom)
        value_list.append(value)
    result = [value_list[-1]]
    for level in range(levels - 2, -1, -1):
        result.append(value_list[level] - upper_list[level] * result[-1])
    return jnp.stack(result[::-1])


def lookup(soil_type, table):
    result = jnp.zeros(soil_type.shape, jnp.float32)
    for klass in range(table.shape[0]):
        result = jnp.where(soil_type == klass, table[klass], result)
    return result


def local(
    pressure,
    sat_old,
    soil_type,
    ks_table,
    alpha_table,
    porosity_table,
    rain,
    evapo,
    land_mask,
    tile,
    cell,
    theta,
    kappa,
):
    depth, size_x, size_y = pressure.shape
    count_x = lax.axis_size("gx")
    count_y = lax.axis_size("gy")
    peers = count_x * count_y
    land = rain.shape[0]
    slots = land // 32
    target = tile[:, 0]
    places = jnp.arange(land, dtype=jnp.int32)
    sorted_target, order = lax.sort((target, places), num_keys=2)
    starts = jnp.searchsorted(sorted_target, jnp.arange(peers, dtype=jnp.int32), side="left")
    rank_sorted = places - starts[sorted_target]
    rank = jnp.zeros((land,), jnp.int32).at[order].set(rank_sorted)
    slot = target * slots + rank
    live = land_mask.astype(jnp.float32)
    payload = jnp.stack([live * rain, live * evapo, cell.astype(jnp.float32)])
    outgoing = jnp.zeros((3, peers * slots), jnp.float32).at[:, slot].set(payload)
    incoming = lax.all_to_all(
        outgoing.reshape(3, peers, slots), ("gx", "gy"), split_axis=1, concat_axis=1, tiled=True
    )
    incoming = incoming.reshape(3, peers * slots)
    position = incoming[2].astype(jnp.int32)
    maps = jnp.zeros((2, size_x * size_y), jnp.float32).at[:, position].add(incoming[:2])
    maps = maps.reshape(2, size_x, size_y)
    decay = jnp.exp(-jnp.arange(depth).astype(jnp.float32) / 2.0)
    rootfrac = decay / jnp.sum(decay)
    top = (jnp.arange(depth) == 0).astype(jnp.float32)
    source = top[:, None, None] * maps[0][None] - rootfrac[:, None, None] * maps[1][None]
    ks = lookup(soil_type, ks_table)
    alpha = lookup(soil_type, alpha_table)
    phi = lookup(soil_type, porosity_table)
    narrow = padded(jnp.stack([pressure, ks, alpha]), (("gx", 2), ("gy", 3)), 1)
    first = residual_core(narrow[0], narrow[1], narrow[2], sat_old, phi, source)
    pressure_next = pressure - 0.8 * first
    widened = padded(pressure_next, (("gx", 1), ("gy", 2)), 1)
    residual_next = residual_core(widened, narrow[1], narrow[2], sat_old, phi, source)
    top_fields = jnp.stack(
        [pressure_next[0], jnp.sqrt(relperm(pressure_next[0], alpha[0]))]
    ).reshape(2, size_x * size_y)
    answer = top_fields[:, position]
    returned = lax.all_to_all(
        answer.reshape(2, peers, slots), ("gx", "gy"), split_axis=1, concat_axis=1, tiled=True
    )
    returned = returned.reshape(2, peers * slots)[:, slot]
    solved = soil_solve(theta, kappa, returned[0], returned[1])
    theta_next = jnp.where(land_mask[None, :] == 1, solved, theta)
    return (pressure_next, residual_next, theta_next)


def solution(mesh):
    in_specs = (
        P(None, "gx", "gy"),
        P(None, "gx", "gy"),
        P(None, "gx", "gy"),
        P(),
        P(),
        P(),
        P(("gx", "gy")),
        P(("gx", "gy")),
        P(("gx", "gy")),
        P(("gx", "gy"), None),
        P(("gx", "gy")),
        P(None, ("gx", "gy")),
        P(None, ("gx", "gy")),
    )
    out_specs = (P(None, "gx", "gy"), P(None, "gx", "gy"), P(None, ("gx", "gy")))
    return jax.shard_map(local, mesh=mesh, in_specs=in_specs, out_specs=out_specs, check_vma=False)
```

profile of v0, /device:TPU:0, one launch (start us, length us, event | category | flops | bytes accessed | tf_op | source)
XLA Modules:
  0.0 325.5 jit_solution(15237836965860060548)
XLA Ops:
  0.7 7.1 %sort.15 = (s32[8192]{0:T(1024)S(1)}, s32[8192]{0:T(1024)S(1)}) sort(s32[8192]{0:T(1024)} %bitcast.132, s32[8192]{0:T(1024)S(1)} %iota.21), dimensions={0}, to_apply=%region_0.0 | sort | flops 106496 | bytes 131072 | tf_op jit(solution)/shard_map/sort | solution.py:110
  7.8 10.5 %while.24 = (s32[]{:T(128)}, u32[32]{0:T(128)S(1)}, u32[32]{0:T(128)S(1)}, s32[8192]{0:T(1024)S(1)}, s32[]{:T(128)}, /*index=5*/s32[]{:T(128)}, s32[]{}) while((s32[]{:T(128)}, u32[32]{0:T(128)S(1)}, u32[32]{0:T(128)S(1)}, s32[8192]{0:T(1024)S(1)}, s32[]{:T(128)}, /*index=5*/s32[]{:T(128)}, s32[]{}) %tuple.161), condition=%wide.region_2.3_spmd.clone, body=%wide.region_1.2_spmd.clone.sunk | while | flops 1444 | bytes 5732 | solution.py:111
  7.9 0.7 gather_fusion
  8.6 0.7 gather_fusion
  9.4 0.7 gather_fusion
  10.1 0.7 gather_fusion
  10.9 0.7 gather_fusion
  11.6 0.7 gather_fusion
  12.4 0.7 gather_fusion
  13.1 0.7 gather_fusion
  13.9 0.7 gather_fusion
  14.6 0.7 gather_fusion
  15.4 0.7 gather_fusion
  16.1 0.7 gather_fusion
  16.9 0.7 gather_fusion
  17.7 0.7 gather_fusion
  18.4 0.7 fusion.87
  19.1 0.7 fusion.88
  19.8 20.2 %select_subtract_fusion = s32[8192]{0:T(1024)S(1)} fusion(s32[8192]{0:T(1024)S(1)} %get-tuple-element.297, s32[]{:T(128)} %bitcast.46, s32[]{:T(128)} %bitcast.47, s32[]{:T(128)} %bitcast.48, s32[]{:T(128)} %bitcast.49, s32[]{:T(128)} %bitcast.50, s32[]{:T(128)} %bitcast.51, s32[]{:T(128)} %bitcast.52, s32[]{:T(128)} %bitcast.53, s32[]{:T(128)} %bitcast.54, ...), kind=kLoop, calls=%fused_computation.161 | loop fusion | flops 540672 | bytes 65664 | tf_op jit(solution)/shard_map/sub | solution.py:112
  40.0 30.5 %scatter_custom_fusion = s32[8192]{0:T(1024)S(1)} fusion(s32[8192]{0:T(1024)S(1)} %compare_select_fusion.8, s32[8192]{0:T(1024)S(1)} %select_subtract_fusion, s32[]{:T(128)} %constant.41.clone.1), kind=kCustom, calls=%fused_computation.203 | custom fusion | bytes 32772 | tf_op jit(solution)/shard_map/scatter | solution.py:113
  71.2 2.7 copy.196
  73.9 23.0 %scatter_custom_fusion.1 = f32[3,8192]{0,1:T(8,128)} fusion(s32[8192]{0:T(1024)S(1)} %get-tuple-element.143, f32[8192,3]{1,0:T(8,128)} %copy.196, f32[]{:T(128)} %constant.42.clone.1), kind=kCustom, calls=%fused_computation.17 | custom fusion | bytes 98816 | tf_op jit(solution)/shard_map/scatter | solution.py:117
  97.0 3.5 %copy.197 = f32[3,32,256]{2,0,1:T(4,128)} copy(f32[3,32,256]{0,2,1:T(8,128)} %bitcast.109) | data formatting | bytes 196608 | tf_op jit(solution)/shard_map/reshape | solution.py:119
  100.5 7.4 %all-to-all-start = ((f32[3,32,256]{2,0,1:T(4,128)}), f32[3,32,256]{2,0,1:T(4,128)}, u32[]{:S(2)}, u32[]{:S(2)}) async-start(f32[3,32,256]{2,0,1:T(4,128)} %copy.197), calls=%async_computation | async-start | bytes 262144 | tf_op jit(solution)/shard_map/all_to_all | solution.py:118
  108.0 0.7 fusion.90
  108.7 0.7 fusion.89
  109.4 9.0 %select_bitcast_fusion = (f32[1,10,64,128]{3,2,1,0:T(8,128)S(1)}, pred[10,64,128]{2,1,0:T(8,128)(4,1)S(1)}, pred[10,64,128]{2,1,0:T(8,128)(4,1)S(1)}, pred[10,64...) fusion(f32[]{:T(128)} %bitcast.26, f32[]{:T(128)} %bitcast.25, ...), kind=kLoop, calls=%fused_computation.114 | loop fusion | flops 2129920 | bytes 1720372 | tf_op jit(solution)/shard_map/stack | solution.py:132
  118.5 8.5 %select_select_fusion = f32[10,64,128]{2,1,0:T(8,128)S(1)} fusion(pred[10,64,128]{2,1,0:T(8,128)(4,1)S(1)} %get-tuple-element.159, pred[10,64,128]{2,1,0:T(8,128)(4,1)S(1)} %get-tuple-element.158, pred[10,64,128]{2,1,0:T(8,128)(4,1)S(1)} %get-tuple-element.157, pred[10,64,128]{2,1,0:T(8,128)(4,1)S(1)} %get-tuple-element.156, ...), kind=kLoop, calls=%fused_computation.113 | loop fusion | flops 1064960 | bytes 1392692 | tf_op jit(solution)/shard_map/jit(_where)/select_n | solution.py:83
  127.0 2.1 collective-permute-start
  129.1 1.3 collective-permute-start.1
  131.0 0.7 fusion.86
  134.3 3.4 %collective-permute-start.2 = (f32[3,10,66,1]{2,3,1,0:T(1,128)S(1)}, f32[3,10,66,1]{2,3,1,0:T(1,128)S(1)}, u32[]{:S(2)}, u32[]{:S(2)}) collective-permute-start(f32[3,10,66,1]{2,3,1,0:T(1,128)S(1)} %copy.192), channel_id=1, source_target_pairs={{0,1},{1,2},{2,3},{4,5},{5,6},{6,7},{8,9},{9,10},{10,11},{12,13},{... | collective-permute-start | bytes 23768 | tf_op jit(solution)/shard_map/ppermute | solution.py:12
  138.1 1.5 collective-permute-start.3
  139.6 1.2 broadcast_divide_fusion
  140.8 1.5 copy.194
  142.3 1.4 collective-permute-done.3
  143.7 1.5 copy.195
  145.2 2.6 pad_maximum_fusion
  149.1 1.3 fusion.70
  150.3 0.9 slice.571
  151.3 2.7 copy.198
  153.9 0.9 slice_convert_fusion
  154.9 46.5 %scatter_custom_fusion.2 = f32[2,8192]{0,1:T(8,128)} fusion(s32[8192]{0:T(1024)S(1)} %bitcast.129, f32[8192,2]{1,0:T(8,128)} %copy.198, f32[]{:T(128)} %constant.42.clone.1), kind=kCustom, calls=%fused_computation.19 | custom fusion | flops 16384 | bytes 66048 | tf_op jit(solution)/shard_map/scatter-add | solution.py:123
  201.6 6.9 %slice_reduce_fusion.1 = (f32[8192]{0:T(1024)S(1)}, f32[8192]{0:T(1024)S(1)}) fusion(f32[2,8192]{0,1:T(8,128)} %scatter_custom_fusion.2), kind=kLoop, calls=%fused_computation.15 | loop fusion | bytes 131072 | tf_op jit(solution)/shard_map/slice | solution.py:128
  208.7 10.5 %fusion.53 = (f32[10,64,128]{2,1,0:T(8,128)S(1)}, f32[10,64,128]{2,1,0:T(8,128)}) fusion(f32[10,64,128]{2,1,0:T(8,128)S(1)} %copy-done.7, f32[10,66,130]{2,1,0:T(8,128)S(1)} %copy-done.1, f32[10,66,130]{2,1,0:T(8,128)S(1)} %copy-done.3, f32[9,64,128]{2,1,0:T(8,128)S(1)} %copy-done.12, f32[10,64,128]{2,1,0:T(8,128)S(1)} %copy-done.9, ...), kind=kLoop, calls=%fused_computation.91 | loop fusion | flops 6717440 | bytes 7651460 | tf_op jit(solution)/shard_map/sub | solution.py:134
  219.3 0.8 fusion.84
  220.1 2.9 collective-permute-start.4
  223.0 1.3 collective-permute-start.5
  224.4 3.8 %collective-permute-done.5 = f32[10,1,128]{2,1,0:T(1,128)S(1)} collective-permute-done((f32[10,1,128]{2,1,0:T(1,128)S(1)}, f32[10,1,128]{2,1,0:T(1,128)S(1)}, u32[]{:S(2)}, u32[]{:S(2)}) %collective-permute-start.5) | collective-permute-done | bytes 5152 | tf_op jit(solution)/shard_map/ppermute | solution.py:15
  228.3 1.0 fusion.83
  229.2 4.1 %collective-permute-start.6 = (f32[10,66,1]{2,1,0:T(8,128)}, f32[10,66,1]{2,1,0:T(8,128)}, u32[]{:S(2)}, u32[]{:S(2)}) collective-permute-start(f32[10,66,1]{2,1,0:T(8,128)} %get-tuple-element.168), channel_id=1, source_target_pairs={{0,1},{1,2},{2,3},{4,5},{5,6},{6,7},{8,9},{9,10},{10,11},{12,13},{... | collective-permute-start | bytes 7928 | tf_op jit(solution)/shard_map/ppermute | solution.py:12
  233.3 1.3 collective-permute-start.7
  234.7 2.7 copy.199
  237.4 29.9 %gather_fusion.1 = f32[8192,2]{1,0:T(8,128)} fusion(f32[2,8192]{0,1:T(8,128)} %copy.199, s32[8192]{0:T(1024)S(1)} %broadcast_clamp_fusion.1), kind=kCustom, calls=%fused_computation.1 | custom fusion | bytes 163840 | tf_op jit(solution)/shard_map/gather | solution.py:140
  267.2 3.4 %copy.200 = f32[2,32,256]{2,0,1:T(2,128)} copy(f32[2,32,256]{0,2,1:T(8,128)} %bitcast.117) | data formatting | bytes 131072 | tf_op jit(solution)/shard_map/reshape | solution.py:142
  270.7 8.9 %all-to-all-start.1 = ((f32[2,32,256]{2,0,1:T(2,128)}), f32[2,32,256]{2,0,1:T(2,128)S(1)}, u32[]{:S(2)}, u32[]{:S(2)}) async-start(f32[2,32,256]{2,0,1:T(2,128)} %copy.200), calls=%async_computation.1 | async-start | bytes 131072 | tf_op jit(solution)/shard_map/all_to_all | solution.py:141
  279.7 1.6 fusion.12
  281.7 3.3 %fusion.32 = f32[10,64,128]{2,1,0:T(8,128)} fusion(f32[10,64,128]{2,1,0:T(8,128)S(1)} %get-tuple-element.144, f32[10,66,1]{2,1,0:T(8,128)} %collective-permute-done.7, f32[10,1,128]{2,1,0:T(1,128)S(1)} %collective-permute-done.5, f32[10,1,128]{2,1,0:T(1,128)S(1)} %collective-permute-done.4, f32[10,66,130]{2,1,0:T(8,128)S(1)} %fusion.12, ...), kind=kLoop, calls=%fused_computation.58 | loop fusion | flops 6144000 | bytes 4963568 | tf_op jit(solution)/shard_map/sub | solution.py:54
  285.0 1.9 all-to-all-done.1
  286.9 2.7 copy.201
  289.5 29.9 %gather_fusion.2 = f32[8192,2]{1,0:T(8,128)} fusion(f32[2,8192]{0,1:T(8,128)} %bitcast.113, s32[8192]{0:T(1024)S(1)} %copy-done.38), kind=kCustom, calls=%fused_computation.2 | custom fusion | bytes 163840 | tf_op jit(solution)/shard_map/gather | solution.py:144
  319.4 2.9 copy.202
  322.5 0.7 negate_divide_fusion
  324.7 0.8 broadcast_select_fusion.2
  (185 shorter events, 8.2 us)
Async XLA Ops:
  0.6 69.8 %copy-start.41 = (s32[8192,1]{0,1:T(1,128)S(1)}, s32[8192,1]{0,1:T(1,128)}, u32[]{:S(2)}) copy-start(s32[8192,1]{0,1:T(1,128)} %param.24) | copy-start | bytes 98308
  0.6 70.4 %copy-start.48 = (s32[8192]{0:T(1024)S(1)}, s32[8192]{0:T(1024)}, u32[]{:S(2)}) copy-start(s32[8192]{0:T(1024)} %param.25) | copy-start | bytes 98308
  0.7 70.4 %copy-start.46 = (f32[8192]{0:T(1024)S(1)}, f32[8192]{0:T(1024)}, u32[]{:S(2)}) copy-start(f32[8192]{0:T(1024)} %param.21) | copy-start | bytes 98308
  0.7 70.4 %copy-start.47 = (f32[8192]{0:T(1024)S(1)}, f32[8192]{0:T(1024)}, u32[]{:S(2)}) copy-start(f32[8192]{0:T(1024)} %param.22) | copy-start | bytes 98308
  0.7 70.4 %copy-start.37 = (s32[8192]{0:T(1024)S(1)}, s32[8192]{0:T(1024)}, u32[]{:S(2)}) copy-start(s32[8192]{0:T(1024)} %param.23) | copy-start | bytes 98308
  97.0 11.0 %copy-start.42 = (f32[13]{0:T(128)S(1)}, f32[13]{0:T(128)}, u32[]{:S(2)}) copy-start(f32[13]{0:T(128)} %param.18) | copy-start | bytes 160
  97.0 11.7 %copy-start.43 = (f32[13]{0:T(128)S(1)}, f32[13]{0:T(128)}, u32[]{:S(2)}) copy-start(f32[13]{0:T(128)} %param.19) | copy-start | bytes 160
  97.0 12.4 %copy-start.34 = (s32[10,64,128]{2,1,0:T(8,128)S(1)}, s32[10,64,128]{2,1,0:T(8,128)}, u32[]{:S(2)}) copy-start(s32[10,64,128]{2,1,0:T(8,128)} %param.17) | copy-start | bytes 983044
  100.5 26.5 %copy-start.6 = (f32[10,64,128]{2,1,0:T(8,128)S(1)}, f32[10,64,128]{2,1,0:T(8,128)}, u32[]{:S(2)}) copy-start(f32[10,64,128]{2,1,0:T(8,128)} %param.15) | copy-start | bytes 983044
  100.5 49.8 %all-to-all-start = ((f32[3,32,256]{2,0,1:T(4,128)}), f32[3,32,256]{2,0,1:T(4,128)}, u32[]{:S(2)}, u32[]{:S(2)}) async-start(f32[3,32,256]{2,0,1:T(4,128)} %copy.197), calls=%async_computation | async-start | bytes 262144 | tf_op jit(solution)/shard_map/all_to_all | solution.py:118
  107.9 23.1 %copy-start.44 = (f32[13]{0:T(128)S(1)}, f32[13]{0:T(128)}, u32[]{:S(2)}) copy-start(f32[13]{0:T(128)} %param.20) | copy-start | bytes 160
  118.4 15.0 %copy-start.13 = (pred[10,64,128]{2,1,0:T(8,128)(4,1)}, pred[10,64,128]{2,1,0:T(8,128)(4,1)S(1)}, u32[]{:S(2)}) copy-start(pred[10,64,128]{2,1,0:T(8,128)(4,1)S(1)} %get-tuple-element.150) | copy-start | bytes 245764
  118.4 15.0 %copy-start.15 = (pred[10,64,128]{2,1,0:T(8,128)(4,1)}, pred[10,64,128]{2,1,0:T(8,128)(4,1)S(1)}, u32[]{:S(2)}) copy-start(pred[10,64,128]{2,1,0:T(8,128)(4,1)S(1)} %get-tuple-element.151) | copy-start | bytes 245764
  118.4 15.0 %copy-start.17 = (pred[10,64,128]{2,1,0:T(8,128)(4,1)}, pred[10,64,128]{2,1,0:T(8,128)(4,1)S(1)}, u32[]{:S(2)}) copy-start(pred[10,64,128]{2,1,0:T(8,128)(4,1)S(1)} %get-tuple-element.152) | copy-start | bytes 245764
  118.4 14.9 %copy-start.19 = (pred[10,64,128]{2,1,0:T(8,128)(4,1)}, pred[10,64,128]{2,1,0:T(8,128)(4,1)S(1)}, u32[]{:S(2)}) copy-start(pred[10,64,128]{2,1,0:T(8,128)(4,1)S(1)} %get-tuple-element.153) | copy-start | bytes 245764
  118.4 14.9 %copy-start.21 = (pred[10,64,128]{2,1,0:T(8,128)(4,1)}, pred[10,64,128]{2,1,0:T(8,128)(4,1)S(1)}, u32[]{:S(2)}) copy-start(pred[10,64,128]{2,1,0:T(8,128)(4,1)S(1)} %get-tuple-element.154) | copy-start | bytes 245764
  118.4 14.9 %copy-start.23 = (pred[10,64,128]{2,1,0:T(8,128)(4,1)}, pred[10,64,128]{2,1,0:T(8,128)(4,1)S(1)}, u32[]{:S(2)}) copy-start(pred[10,64,128]{2,1,0:T(8,128)(4,1)S(1)} %get-tuple-element.155) | copy-start | bytes 245764
  118.4 14.9 %copy-start.25 = (pred[10,64,128]{2,1,0:T(8,128)(4,1)}, pred[10,64,128]{2,1,0:T(8,128)(4,1)S(1)}, u32[]{:S(2)}) copy-start(pred[10,64,128]{2,1,0:T(8,128)(4,1)S(1)} %get-tuple-element.156) | copy-start | bytes 245764
  118.4 14.9 %copy-start.27 = (pred[10,64,128]{2,1,0:T(8,128)(4,1)}, pred[10,64,128]{2,1,0:T(8,128)(4,1)S(1)}, u32[]{:S(2)}) copy-start(pred[10,64,128]{2,1,0:T(8,128)(4,1)S(1)} %get-tuple-element.157) | copy-start | bytes 245764
  118.4 14.9 %copy-start.29 = (pred[10,64,128]{2,1,0:T(8,128)(4,1)}, pred[10,64,128]{2,1,0:T(8,128)(4,1)S(1)}, u32[]{:S(2)}) copy-start(pred[10,64,128]{2,1,0:T(8,128)(4,1)S(1)} %get-tuple-element.158) | copy-start | bytes 245764
  118.4 14.9 %copy-start.31 = (pred[10,64,128]{2,1,0:T(8,128)(4,1)}, pred[10,64,128]{2,1,0:T(8,128)(4,1)S(1)}, u32[]{:S(2)}) copy-start(pred[10,64,128]{2,1,0:T(8,128)(4,1)S(1)} %get-tuple-element.159) | copy-start | bytes 245764
  127.0 18.3 %copy-start.5 = (f32[10,64,128]{2,1,0:T(8,128)}, f32[10,64,128]{2,1,0:T(8,128)S(1)}, u32[]{:S(2)}) copy-start(f32[10,64,128]{2,1,0:T(8,128)S(1)} %select_select_fusion) | copy-start | bytes 983044
  127.0 5.9 %collective-permute-start = (f32[3,10,1,128]{3,2,1,0:T(1,128)S(1)}, f32[3,10,1,128]{3,2,1,0:T(1,128)S(1)}, u32[]{:S(2)}, u32[]{:S(2)}) collective-permute-start(f32[3,10,1,128]{3,2,1,0:T(1,128)S(1)} %get-tuple-element.166), channel_id=1, source_target_pairs={{0,4},{4,8},{8,12},{12,16},{16,20},{20,24},{24,28},{1,5},{5,9},{9,... | collective-permute-start | bytes 46088 | tf_op jit(solution)/shard_map/ppermute | solution.py:12
  129.1 4.2 %collective-permute-start.1 = (f32[3,10,1,128]{3,2,1,0:T(1,128)S(1)}, f32[3,10,1,128]{3,2,1,0:T(1,128)S(1)}, u32[]{:S(2)}, u32[]{:S(2)}) collective-permute-start(f32[3,10,1,128]{3,2,1,0:T(1,128)S(1)} %get-tuple-element.167), channel_id=1, source_target_pairs={{4,0},{8,4},{12,8},{16,12},{20,16},{24,20},{28,24},{5,1},{9,5},{13... | collective-permute-start | bytes 46088 | tf_op jit(solution)/shard_map/ppermute | solution.py:15
  134.3 6.5 %collective-permute-start.2 = (f32[3,10,66,1]{2,3,1,0:T(1,128)S(1)}, f32[3,10,66,1]{2,3,1,0:T(1,128)S(1)}, u32[]{:S(2)}, u32[]{:S(2)}) collective-permute-start(f32[3,10,66,1]{2,3,1,0:T(1,128)S(1)} %copy.192), channel_id=1, source_target_pairs={{0,1},{1,2},{2,3},{4,5},{5,6},{6,7},{8,9},{9,10},{10,11},{12,13},{... | collective-permute-start | bytes 23768 | tf_op jit(solution)/shard_map/ppermute | solution.py:12
  138.1 5.6 %collective-permute-start.3 = (f32[3,10,66,1]{2,3,1,0:T(1,128)S(1)}, f32[3,10,66,1]{2,3,1,0:T(1,128)S(1)}, u32[]{:S(2)}, u32[]{:S(2)}) collective-permute-start(f32[3,10,66,1]{2,3,1,0:T(1,128)S(1)} %copy.193), channel_id=1, source_target_pairs={{1,0},{2,1},{3,2},{5,4},{6,5},{7,6},{9,8},{10,9},{11,10},{13,12},{... | collective-permute-start | bytes 23768 | tf_op jit(solution)/shard_map/ppermute | solution.py:15
  148.0 0.9 copy-start
  148.1 0.9 copy-start.2
  154.9 53.6 %copy-start.39 = (s32[8192,1]{0,1:T(1,128)}, s32[8192,1]{0,1:T(1,128)S(1)}, u32[]{:S(2)}) copy-start(s32[8192,1]{0,1:T(1,128)S(1)} %compare_select_fusion.5) | copy-start | bytes 98308
  201.5 7.1 %copy-start.1 = (f32[10,66,130]{2,1,0:T(8,128)S(1)}, f32[10,66,130]{2,1,0:T(8,128)}, u32[]{:S(2)}) copy-start(f32[10,66,130]{2,1,0:T(8,128)} %copy-done) | copy-start | bytes 1029604
  201.5 7.1 %copy-start.3 = (f32[10,66,130]{2,1,0:T(8,128)S(1)}, f32[10,66,130]{2,1,0:T(8,128)}, u32[]{:S(2)}) copy-start(f32[10,66,130]{2,1,0:T(8,128)} %copy-done.2) | copy-start | bytes 1029604
  201.5 7.1 %copy-start.7 = (f32[10,64,128]{2,1,0:T(8,128)S(1)}, f32[10,64,128]{2,1,0:T(8,128)}, u32[]{:S(2)}) copy-start(f32[10,64,128]{2,1,0:T(8,128)} %param.15) | copy-start | bytes 983044
  201.5 7.1 %copy-start.9 = (f32[10,64,128]{2,1,0:T(8,128)S(1)}, f32[10,64,128]{2,1,0:T(8,128)}, u32[]{:S(2)}) copy-start(f32[10,64,128]{2,1,0:T(8,128)} %param.16) | copy-start | bytes 983044
  201.5 7.1 %copy-start.12 = (f32[9,64,128]{2,1,0:T(8,128)S(1)}, f32[9,64,128]{2,1,0:T(8,128)}, u32[]{:S(2)}) copy-start(f32[9,64,128]{2,1,0:T(8,128)} %fusion.70) | copy-start | bytes 884740
  201.5 7.1 %copy-start.14 = (pred[10,64,128]{2,1,0:T(8,128)(4,1)S(1)}, pred[10,64,128]{2,1,0:T(8,128)(4,1)}, u32[]{:S(2)}) copy-start(pred[10,64,128]{2,1,0:T(8,128)(4,1)} %copy-done.13) | copy-start | bytes 245764
  201.5 7.1 %copy-start.16 = (pred[10,64,128]{2,1,0:T(8,128)(4,1)S(1)}, pred[10,64,128]{2,1,0:T(8,128)(4,1)}, u32[]{:S(2)}) copy-start(pred[10,64,128]{2,1,0:T(8,128)(4,1)} %copy-done.15) | copy-start | bytes 245764
  201.5 7.1 %copy-start.18 = (pred[10,64,128]{2,1,0:T(8,128)(4,1)S(1)}, pred[10,64,128]{2,1,0:T(8,128)(4,1)}, u32[]{:S(2)}) copy-start(pred[10,64,128]{2,1,0:T(8,128)(4,1)} %copy-done.17) | copy-start | bytes 245764
  201.5 7.1 %copy-start.20 = (pred[10,64,128]{2,1,0:T(8,128)(4,1)S(1)}, pred[10,64,128]{2,1,0:T(8,128)(4,1)}, u32[]{:S(2)}) copy-start(pred[10,64,128]{2,1,0:T(8,128)(4,1)} %copy-done.19) | copy-start | bytes 245764
  201.5 7.1 %copy-start.22 = (pred[10,64,128]{2,1,0:T(8,128)(4,1)S(1)}, pred[10,64,128]{2,1,0:T(8,128)(4,1)}, u32[]{:S(2)}) copy-start(pred[10,64,128]{2,1,0:T(8,128)(4,1)} %copy-done.21) | copy-start | bytes 245764
  201.5 7.1 %copy-start.24 = (pred[10,64,128]{2,1,0:T(8,128)(4,1)S(1)}, pred[10,64,128]{2,1,0:T(8,128)(4,1)}, u32[]{:S(2)}) copy-start(pred[10,64,128]{2,1,0:T(8,128)(4,1)} %copy-done.23) | copy-start | bytes 245764
  201.6 7.1 %copy-start.26 = (pred[10,64,128]{2,1,0:T(8,128)(4,1)S(1)}, pred[10,64,128]{2,1,0:T(8,128)(4,1)}, u32[]{:S(2)}) copy-start(pred[10,64,128]{2,1,0:T(8,128)(4,1)} %copy-done.25) | copy-start | bytes 245764
  201.6 7.1 %copy-start.28 = (pred[10,64,128]{2,1,0:T(8,128)(4,1)S(1)}, pred[10,64,128]{2,1,0:T(8,128)(4,1)}, u32[]{:S(2)}) copy-start(pred[10,64,128]{2,1,0:T(8,128)(4,1)} %copy-done.27) | copy-start | bytes 245764
  201.6 7.1 %copy-start.30 = (pred[10,64,128]{2,1,0:T(8,128)(4,1)S(1)}, pred[10,64,128]{2,1,0:T(8,128)(4,1)}, u32[]{:S(2)}) copy-start(pred[10,64,128]{2,1,0:T(8,128)(4,1)} %copy-done.29) | copy-start | bytes 245764
  201.6 7.1 %copy-start.32 = (pred[10,64,128]{2,1,0:T(8,128)(4,1)S(1)}, pred[10,64,128]{2,1,0:T(8,128)(4,1)}, u32[]{:S(2)}) copy-start(pred[10,64,128]{2,1,0:T(8,128)(4,1)} %copy-done.31) | copy-start | bytes 245764
  201.6 7.1 %copy-start.49 = (f32[10]{0:T(128)S(1)}, f32[10]{0:T(128)}, u32[]{:S(2)}) copy-start(f32[10]{0:T(128)} %compare_convert_fusion) | copy-start | bytes 124
  201.6 7.1 %copy-start.51 = (f32[10]{0:T(128)S(1)}, f32[10]{0:T(128)}, u32[]{:S(2)}) copy-start(f32[10]{0:T(128)} %broadcast_divide_fusion) | copy-start | bytes 124
  208.6 10.7 %copy-start.35 = (f32[8192]{0:T(1024)}, f32[8192]{0:T(1024)S(1)}, u32[]{:S(2)}) copy-start(f32[8192]{0:T(1024)S(1)} %get-tuple-element.97) | copy-start | bytes 98308
  219.3 62.4 %copy-start.4 = (f32[10,64,128]{2,1,0:T(8,128)}, f32[10,64,128]{2,1,0:T(8,128)S(1)}, u32[]{:S(2)}) copy-start(f32[10,64,128]{2,1,0:T(8,128)S(1)} %get-tuple-element.144) | copy-start | bytes 983044
  219.3 15.4 %copy-start.40 = (s32[8192,1]{0,1:T(1,128)S(1)}, s32[8192,1]{0,1:T(1,128)}, u32[]{:S(2)}) copy-start(s32[8192,1]{0,1:T(1,128)} %copy-done.39) | copy-start | bytes 98308
  220.1 4.3 %collective-permute-start.4 = (f32[10,1,128]{2,1,0:T(1,128)S(1)}, f32[10,1,128]{2,1,0:T(1,128)S(1)}, u32[]{:S(2)}, u32[]{:S(2)}) collective-permute-start(f32[10,1,128]{2,1,0:T(1,128)S(1)} %get-tuple-element.172), channel_id=1, source_target_pairs={{0,4},{4,8},{8,12},{12,16},{16,20},{20,24},{24,28},{1,5},{5,9},{9,... | collective-permute-start | bytes 15368 | tf_op jit(solution)/shard_map/ppermute | solution.py:12
  223.0 5.2 %collective-permute-start.5 = (f32[10,1,128]{2,1,0:T(1,128)S(1)}, f32[10,1,128]{2,1,0:T(1,128)S(1)}, u32[]{:S(2)}, u32[]{:S(2)}) collective-permute-start(f32[10,1,128]{2,1,0:T(1,128)S(1)} %get-tuple-element.173), channel_id=1, source_target_pairs={{4,0},{8,4},{12,8},{16,12},{20,16},{24,20},{28,24},{5,1},{9,5},{13... | collective-permute-start | bytes 15368 | tf_op jit(solution)/shard_map/ppermute | solution.py:15
  229.2 50.4 %collective-permute-start.6 = (f32[10,66,1]{2,1,0:T(8,128)}, f32[10,66,1]{2,1,0:T(8,128)}, u32[]{:S(2)}, u32[]{:S(2)}) collective-permute-start(f32[10,66,1]{2,1,0:T(8,128)} %get-tuple-element.168), channel_id=1, source_target_pairs={{0,1},{1,2},{2,3},{4,5},{5,6},{6,7},{8,9},{9,10},{10,11},{12,13},{... | collective-permute-start | bytes 7928 | tf_op jit(solution)/shard_map/ppermute | solution.py:12
  233.3 46.3 %collective-permute-start.7 = (f32[10,66,1]{2,1,0:T(8,128)}, f32[10,66,1]{2,1,0:T(8,128)}, u32[]{:S(2)}, u32[]{:S(2)}) collective-permute-start(f32[10,66,1]{2,1,0:T(8,128)} %get-tuple-element.169), channel_id=1, source_target_pairs={{1,0},{2,1},{3,2},{5,4},{6,5},{7,6},{9,8},{10,9},{11,10},{13,12},{... | collective-permute-start | bytes 7928 | tf_op jit(solution)/shard_map/ppermute | solution.py:15
  270.7 16.2 %all-to-all-start.1 = ((f32[2,32,256]{2,0,1:T(2,128)}), f32[2,32,256]{2,0,1:T(2,128)S(1)}, u32[]{:S(2)}, u32[]{:S(2)}) async-start(f32[2,32,256]{2,0,1:T(2,128)} %copy.200), calls=%async_computation.1 | async-start | bytes 131072 | tf_op jit(solution)/shard_map/all_to_all | solution.py:141
  279.6 2.0 copy-start.10
  279.6 2.0 copy-start.11
  279.6 2.0 copy-start.36
  279.6 2.0 copy-start.50
  279.6 2.0 copy-start.52
  285.0 4.6 %copy-start.38 = (s32[8192]{0:T(1024)S(1)}, s32[8192]{0:T(1024)}, u32[]{:S(2)}) copy-start(s32[8192]{0:T(1024)} %get-tuple-element.142) | copy-start | bytes 98308
  319.4 3.0 copy-start.33
  319.4 3.8 %copy-start.8 = (f32[10,8192]{1,0:T(8,128)S(1)}, f32[10,8192]{1,0:T(8,128)}, u32[]{:S(2)}) copy-start(f32[10,8192]{1,0:T(8,128)} %param.26) | copy-start | bytes 983044
  322.5 2.2 copy-start.45
where the time goes:
time: 327 us; the launch traced here: 326 us
  local copies, waits for them, and re-layouts  162 us (50%)
  other arithmetic  120 us (37%)
  starting transfers between devices  34.2 us (10%)
  waiting for transfers between devices  7.59 us (2%)
    scatter-add x1, other arithmetic, local(): jnp.zeros((2, size_x * size_y), jnp.float32).at[:, position]  46.5 us
    gather x2, local copies, waits for them, and re-layouts, local(): returned = returned.reshape(2, peers * slots)[:, slot]  32.8 us
    scatter x1, local copies, waits for them, and re-layouts, local(): rank = jnp.zeros((land,), jnp.int32).at[order].set(rank_sorted)  30.5 us
    gather x1, local copies, waits for them, and re-layouts, local(): answer = top_fields[:, position]  29.9 us
    scatter x1, local copies, waits for them, and re-layouts, local(): jnp.zeros((3, peers * slots), jnp.float32).at[:, slot].set(payload)  23 us
    sub x1, other arithmetic, local(): rank_sorted = places - starts[sorted_target]  20.2 us
    ppermute x4, starting transfers between devices, padded(): lax.ppermute(lax.slice_in_dim(block, block.shape[dim] - width, None, axis...  12.5 us
    sub x1, other arithmetic, local(): pressure_next = pressure - 0.8 * first  10.5 us
  transfers between devices with their start and end apart: 10, of which 4 were waited for; matrix products, arithmetic and copies ran while one was open for 22% of the time, Pallas kernels for 0%

commit v1 on v0

v1 whole, which is shorter than its diff:
```python
import functools
import math

import jax
import jax.numpy as jnp
from jax import lax
from jax.experimental import pallas as pl
from jax.experimental.pallas import tpu as pltpu
from jax.sharding import PartitionSpec as P

F32 = jnp.float32
BF16 = jnp.bfloat16
MESH = pl.DeviceIdType.MESH
NT = (((1,), (1,)), ((), ()))
NN = (((1,), (0,)), ((), ()))
GROUP = 8


def dot(a, b, dims):
    return lax.dot_general(a, b, dims, preferred_element_type=F32)


def halves(value):
    high = value.astype(BF16).astype(F32)
    return high, value - high


def relperm(p, alpha):
    head = alpha * jnp.maximum(-p, 0.0)
    return 1.0 / (1.0 + head * head)


def half_mean(first, second):
    product = first * second
    total = first + second
    return jnp.where(product > 0, product / jnp.where(total > 0, total, 1.0), 0.0)


def iota(shape, dim):
    return lax.broadcasted_iota(jnp.int32, shape, dim)


def kernel(
    dims,
    ks_t, al_t, po_t,
    press, sat_old, soil, rain, evapo, mask, tile, cell, theta, kappa,
    p_out, r_out, t_out,
    onehot, acc, send, recv, ans, ret, rank_s,
    ks, al, phi, kr, gx, gy, gz, base, krn, oney, macc,
    own_x, halo_x, own_y, halo_y, own2_x, halo2_x, own2_y, halo2_y, gbx, gby, fbx, fby,
    th_s, ka_s, so_s, top_s,
    send1, recv1, send2, recv2, hs1, hr1, hs2, hr2,
):
    count_x, count_y, slots = dims
    peers = count_x * count_y
    depth, size_x, size_y = press.shape
    levels, land = theta.shape
    rows = land // 128
    parts = slots // 128
    classes = ks_t.shape[0]
    my_x = lax.axis_index("gx")
    my_y = lax.axis_index("gy")
    me = my_x * count_y + my_y

    for ref in (own_x, halo_x, own_y, halo_y, own2_x, halo2_x, own2_y, halo2_y):
        ref[...] = jnp.zeros_like(ref)

    barrier = pltpu.get_barrier_semaphore()

    def greet(i, carry):
        other = lax.rem(me + i, peers)
        pl.semaphore_signal(
            barrier, inc=1, device_id=(other // count_y, lax.rem(other, count_y)), device_id_type=MESH
        )
        return carry

    lax.fori_loop(1, peers, greet, 0)

    row_id = iota((size_x, size_y), 0)
    lane_id = iota((size_x, size_y), 1)

    def properties(z, carry):
        low, high = carry
        kind = soil[z]
        k = jnp.zeros((size_x, size_y), F32)
        a = k
        f = k
        for c in range(classes):
            hit = kind == c
            k = jnp.where(hit, ks_t[c], k)
            a = jnp.where(hit, al_t[c], a)
            f = jnp.where(hit, po_t[c], f)
        p = press[z]
        r = relperm(p, a)
        ks[z] = k
        al[z] = a
        phi[z] = f
        kr[z] = r
        for n, value in enumerate((p, k, r)):
            own_x[0, pl.ds(n * 16 + z, 1), :] = value[:1, :]
            own_x[1, pl.ds(n * 16 + z, 1), :] = value[size_x - 1 :, :]
            here = lane_id == n * 32 + z
            low = jnp.where(here, value[:, :1], low)
            high = jnp.where(here, value[:, size_y - 1 :], high)
        return low, high

    blank = jnp.zeros((size_x, size_y), F32)
    low, high = lax.fori_loop(0, depth, properties, (blank, blank))
    own_y[0] = low
    own_y[1] = high

    pl.semaphore_wait(barrier, peers - 1)

    def sides(src_x, dst_x, src_y, dst_y, sems_s, sems_r):
        plan = (
            (my_x > 0, src_x, dst_x, 0, my_x - 1, my_y),
            (my_x < count_x - 1, src_x, dst_x, 1, my_x + 1, my_y),
            (my_y > 0, src_y, dst_y, 0, my_x, my_y - 1),
            (my_y < count_y - 1, src_y, dst_y, 1, my_x, my_y + 1),
        )
        made = []
        for n, (there, src, dst, side, at_x, at_y) in enumerate(plan):
            mate = n - side + 1 - side
            outward = pltpu.make_async_remote_copy(
                src_ref=src.at[side], dst_ref=dst.at[1 - side],
                send_sem=sems_s.at[n], recv_sem=sems_r.at[mate],
                device_id=(at_x, at_y), device_id_type=MESH,
            )
            inward = pltpu.make_async_remote_copy(
                src_ref=src.at[side], dst_ref=dst.at[side],
                send_sem=sems_s.at[n], recv_sem=sems_r.at[n],
                device_id=(at_x, at_y), device_id_type=MESH,
            )
            made.append((there, outward, inward))
        return made

    first_sides = sides(own_x, halo_x, own_y, halo_y, hs1, hr1)
    for there, outward, _ in first_sides:
        pl.when(there)(outward.start)

    wide = iota((128, 256), 1)
    tall = iota((128, 256), 0)
    before = ((wide >= 128) | (tall < wide)).astype(F32).astype(BF16)
    peer_id = iota((peers, 128), 0)
    slot_id = iota((slots, 128), 0).astype(F32)
    acc[...] = jnp.zeros_like(acc)

    def dispatch(c, count):
        at = pl.ds(pl.multiple_of(c * GROUP, GROUP), GROUP)
        lanes = pl.ds(pl.multiple_of(c * GROUP * 128, 128), GROUP * 128)
        named = tile[at, :]
        live = mask[at, :].astype(F32)
        where_to = cell[at, :].astype(F32)
        cell_x = jnp.floor(where_to * (1.0 / size_y)) * size_y
        values = (
            *halves(live * rain[at, :]), *halves(live * evapo[at, :]), cell_x, where_to - cell_x
        )
        hits = [named[i : i + 1, :] == peer_id for i in range(GROUP)]
        ones = [jnp.where(h, 1.0, 0.0) for h in hits]
        sums = dot(jnp.concatenate(ones, axis=0).astype(BF16), before, NN)
        ranks = []
        for i in range(GROUP):
            part = sums[i * peers : (i + 1) * peers]
            ranks.append(jnp.sum(ones[i] * (part[:, :128] + count), axis=0, keepdims=True))
            count = count + part[:, 128:]
        rank_s[at, :] = jnp.concatenate(ranks, axis=0)
        chosen = jnp.concatenate(
            [jnp.where(r == slot_id, 1.0, 0.0).astype(BF16) for r in ranks], axis=1
        )
        onehot[:, lanes] = chosen
        left = jnp.concatenate(
            [
                jnp.concatenate(
                    [jnp.where(hits[i], v[i : i + 1, :], 0.0) for i in range(GROUP)], axis=1
                ).astype(BF16)
                for v in values
            ],
            axis=0,
        )
        acc[...] += dot(left, chosen, NT)
        return count

    lax.fori_loop(0, rows // GROUP, dispatch, jnp.zeros((peers, 128), F32))
    for v in range(3):
        full = acc[2 * v * peers : (2 * v + 1) * peers] + acc[(2 * v + 1) * peers : (2 * v + 2) * peers]
        for h in range(parts):
            send[pl.ds(v * parts + h, peers, stride=8), :] = full[:, h * 128 : (h + 1) * 128]

    def block(ref, t):
        return ref.at[pl.ds(pl.multiple_of(t * 8, 8), 8)]

    def carry_over(src, dst, sems_s, sems_r, other, landing):
        return pltpu.make_async_remote_copy(
            src_ref=block(src, other), dst_ref=block(dst, landing),
            send_sem=sems_s.at[other], recv_sem=sems_r.at[landing],
            device_id=(other // count_y, lax.rem(other, count_y)), device_id_type=MESH,
        )

    def exchange(src, dst, sems_s, sems_r):
        def step(i, carry):
            other = lax.rem(me + i, peers)
            carry_over(src, dst, sems_s, sems_r, other, me).start()
            return carry

        lax.fori_loop(1, peers, step, 0)
        mine = pl.ds(pl.multiple_of(me * 8, 8), 8)
        dst[mine, :] = src[mine, :]

    def arrive(src, dst, sems_s, sems_r):
        def step(i, carry):
            other = lax.rem(me + i, peers)
            carry_over(src, dst, sems_s, sems_r, other, other).wait_recv()
            return carry

        lax.fori_loop(1, peers, step, 0)

    def sent(src, dst, sems_s, sems_r):
        def step(i, carry):
            other = lax.rem(me + i, peers)
            carry_over(src, dst, sems_s, sems_r, other, me).wait_send()
            return carry

        lax.fori_loop(1, peers, step, 0)

    exchange(send, recv, send1, recv1)

    def spread(j, carry):
        lanes = pl.ds(pl.multiple_of(j * 128, 128), 128)
        for src, dst in ((theta, th_s), (kappa, ka_s)):
            for k in range(levels):
                dst[k, pl.ds(j, 1), :] = src[k : k + 1, lanes]
        return carry

    lax.fori_loop(0, rows, spread, 0)

    def outflow(z, before_z, pr, rel):
        p = pr[z]
        r = rel[z]
        zn = jnp.minimum(z + 1, depth - 1)
        fx = gx[z] * (r + pltpu.roll(r, 1, 0)) * (p - pltpu.roll(p, 1, 0))
        fy = gy[z] * (r + pltpu.roll(r, 1, 1)) * (p - pltpu.roll(p, 1, 1))
        down = gz[z] * (r + rel[zn]) * (p - pr[zn] + 1.0)
        total = (
            fx - pltpu.roll(fx, size_x - 1, 0) + fy - pltpu.roll(fy, size_y - 1, 1) + down - before_z
        )
        return total, down

    def boundary(z):
        total = jnp.where(row_id == 0, fbx[0, pl.ds(z, 1), :], 0.0)
        total = jnp.where(row_id == size_x - 1, fbx[1, pl.ds(z, 1), :], total)
        one = pltpu.roll(fby[0], lax.rem(size_y - z, size_y), 1)
        two = pltpu.roll(fby[1], size_y - 1 - z, 1)
        return total + jnp.where(lane_id == 0, one, 0.0) + jnp.where(lane_id == size_y - 1, two, 0.0)

    def faces(z, carry):
        k = ks[z]
        zn = jnp.minimum(z + 1, depth - 1)
        gx[z] = jnp.where(row_id == 0, 0.0, half_mean(k, pltpu.roll(k, 1, 0)))
        gy[z] = jnp.where(lane_id == 0, 0.0, half_mean(k, pltpu.roll(k, 1, 1)))
        gz[z] = jnp.where(z < depth - 1, half_mean(k, ks[zn]), 0.0)
        total, down = outflow(z, carry, press, kr)
        base[z] = press[z] - 0.8 * (phi[z] * (jnp.sqrt(kr[z]) - sat_old[z]) + 0.5 * total)
        return down

    lax.fori_loop(0, depth, faces, blank)

    for there, _, inward in first_sides:
        pl.when(there)(inward.wait_recv)
    for s in range(2):
        mine, other = own_x[s], halo_x[s]
        gbx[s] = half_mean(mine[16:32], other[16:32])
        fbx[s] = gbx[s] * (mine[32:48] + other[32:48]) * (mine[0:16] - other[0:16])
        mine, other = own_y[s], halo_y[s]
        gby[s] = half_mean(pltpu.roll(mine, size_y - 32, 1), pltpu.roll(other, size_y - 32, 1))
        fby[s] = gby[s] * pltpu.roll(mine + other, size_y - 64, 1) * (mine - other)

    arrive(send, recv, send1, recv1)
    macc[...] = jnp.zeros_like(macc)
    x_id = iota((size_x, 128), 0).astype(F32)
    y_id = iota((size_y, 128), 0).astype(F32)
    srcs = GROUP // parts

    def gather_in(c, carry):
        lanes = pl.ds(pl.multiple_of(c * GROUP * 128, 128), GROUP * 128)
        left = [[] for _ in range(4)]
        right = []
        for i in range(srcs):
            got = recv[pl.ds(pl.multiple_of((c * srcs + i) * 8, 8), 8), :]
            high_v, low_v = halves(got)
            at_x = jnp.floor(got * (1.0 / size_y))
            at_y = got - at_x * size_y
            for h in range(parts):
                n = 2 * parts + h
                hit = at_x[n : n + 1, :] == x_id
                right.append(jnp.where(at_y[n : n + 1, :] == y_id, 1.0, 0.0).astype(BF16))
                for v in range(2):
                    m = v * parts + h
                    left[2 * v].append(jnp.where(hit, high_v[m : m + 1, :], 0.0).astype(BF16))
                    left[2 * v + 1].append(jnp.where(hit, low_v[m : m + 1, :], 0.0).astype(BF16))
        right = jnp.concatenate(right, axis=1)
        oney[:, lanes] = right
        left = jnp.concatenate([jnp.concatenate(l, axis=1) for l in left], axis=0)
        macc[...] += dot(left, right, NT)
        return carry

    lax.fori_loop(0, peers * parts // GROUP, gather_in, 0)
    rain_map = macc[0:size_x] + macc[size_x : 2 * size_x]
    et_map = macc[2 * size_x : 3 * size_x] + macc[3 * size_x : 4 * size_x]

    scale = 1.0 / sum(math.exp(-z / 2.0) for z in range(depth))

    def update(z, carry):
        frac, low, high = carry
        source = jnp.where(z == 0, rain_map, 0.0) - frac * et_map
        p = base[z] - 0.4 * boundary(z) + 0.4 * source
        r = relperm(p, al[z])
        p_out[z] = p
        krn[z] = r
        for n, value in enumerate((p, r)):
            own2_x[0, pl.ds(n * 16 + z, 1), :] = value[:1, :]
            own2_x[1, pl.ds(n * 16 + z, 1), :] = value[size_x - 1 :, :]
            here = lane_id == n * 32 + z
            low = jnp.where(here, value[:, :1], low)
            high = jnp.where(here, value[:, size_y - 1 :], high)
        return frac * math.exp(-0.5), low, high

    _, low, high = lax.fori_loop(0, depth, update, (jnp.float32(scale), blank, blank))
    own2_y[0] = low
    own2_y[1] = high
    second_sides = sides(own2_x, halo2_x, own2_y, halo2_y, hs2, hr2)
    for there, outward, _ in second_sides:
        pl.when(there)(outward.start)

    fields = []
    for field in (p_out[0], jnp.sqrt(krn[0])):
        high_v, low_v = halves(field)
        fields.append(jnp.concatenate([high_v, low_v], axis=1))
    top_s[...] = jnp.concatenate(fields, axis=0).astype(BF16)

    def answer(c, carry):
        lanes = pl.ds(pl.multiple_of(c * GROUP * 128, 128), GROUP * 128)
        right = oney[:, lanes]
        picked = dot(top_s[...], jnp.concatenate([right, right], axis=0), NN)
        for i in range(srcs):
            at = pl.ds(pl.multiple_of((c * srcs + i) * 8, 8), 8)
            at_x = jnp.floor(recv[at, :] * (1.0 / size_y))
            out = [None] * (2 * parts)
            for h in range(parts):
                n = 2 * parts + h
                hit = at_x[n : n + 1, :] == x_id
                j = (i * parts + h) * 128
                for v in range(2):
                    out[v * parts + h] = jnp.sum(
                        jnp.where(hit, picked[v * size_x : (v + 1) * size_x, j : j + 128], 0.0),
                        axis=0, keepdims=True,
                    )
            out.append(jnp.zeros((8 - 2 * parts, 128), F32))
            ans[at, :] = jnp.concatenate(out, axis=0)
        return carry

    lax.fori_loop(0, peers * parts // GROUP, answer, 0)
    exchange(ans, ret, send2, recv2)

    for there, _, inward in second_sides:
        pl.when(there)(inward.wait_recv)
    for s in range(2):
        mine, other = own2_x[s], halo2_x[s]
        fbx[s] = gbx[s] * (mine[16:32] + other[16:32]) * (mine[0:16] - other[0:16])
        mine, other = own2_y[s], halo2_y[s]
        fby[s] = gby[s] * pltpu.roll(mine + other, size_y - 32, 1) * (mine - other)

    def residual(z, carry):
        frac, previous = carry
        total, down = outflow(z, previous, p_out, krn)
        source = jnp.where(z == 0, rain_map, 0.0) - frac * et_map
        r_out[z] = phi[z] * (jnp.sqrt(krn[z]) - sat_old[z]) + 0.5 * (total + boundary(z)) - 0.5 * source
        return frac * math.exp(-0.5), down

    lax.fori_loop(0, depth, residual, (jnp.float32(scale), blank))

    arrive(ans, ret, send2, recv2)
    tops = []
    for v in range(2):
        value = jnp.concatenate(
            [ret[pl.ds(v * parts + h, peers, stride=8), :] for h in range(parts)], axis=1
        )
        tops.extend(halves(value))
    tops = jnp.concatenate(tops, axis=0).astype(BF16)

    def solve(c, carry):
        at = pl.ds(pl.multiple_of(c * GROUP, GROUP), GROUP)
        lanes = pl.ds(pl.multiple_of(c * GROUP * 128, 128), GROUP * 128)
        named = tile[at, :]
        picked = dot(tops, onehot[:, lanes], NN)
        both = []
        for v in range(2):
            value = picked[2 * v * peers : (2 * v + 1) * peers]
            value = value + picked[(2 * v + 1) * peers : (2 * v + 2) * peers]
            both.append(
                jnp.concatenate(
                    [
                        jnp.sum(
                            jnp.where(
                                named[i : i + 1, :] == peer_id, value[:, i * 128 : (i + 1) * 128], 0.0
                            ),
                            axis=0, keepdims=True,
                        )
                        for i in range(GROUP)
                    ],
                    axis=0,
                )
            )
        p_top, s_top = both
        active = mask[at, :] == 1
        coeff = [ka_s[k, at, :] * (0.5 + s_top) for k in range(levels)]
        coeff.append(jnp.zeros_like(p_top))
        upper, value = [], []
        for k in range(levels):
            diag = 1.0 + coeff[k] + coeff[k + 1]
            right = th_s[k, at, :]
            if k == 0:
                right = right + coeff[0] * p_top
            else:
                diag = diag - coeff[k] * upper[-1]
                right = right + coeff[k] * value[-1]
            inverse = 1.0 / diag
            upper.append(coeff[k + 1] * inverse)
            value.append(right * inverse)
        result = value[-1]
        so_s[levels - 1, at, :] = jnp.where(active, result, th_s[levels - 1, at, :])
        for k in range(levels - 2, -1, -1):
            result = value[k] + upper[k] * result
            so_s[k, at, :] = jnp.where(active, result, th_s[k, at, :])
        return carry

    lax.fori_loop(0, rows // GROUP, solve, 0)

    def collect(j, carry):
        lanes = pl.ds(pl.multiple_of(j * 128, 128), 128)
        for k in range(levels):
            t_out[k : k + 1, lanes] = so_s[k, pl.ds(j, 1), :]
        return carry

    lax.fori_loop(0, rows, collect, 0)

    sent(send, recv, send1, recv1)
    sent(ans, ret, send2, recv2)
    for made in (first_sides, second_sides):
        for there, outward, _ in made:
            pl.when(there)(outward.wait_send)


def local(dims, pressure, sat_old, soil_type, ks_table, alpha_table, porosity_table,
          rain, evapo, land_mask, tile, cell, theta, kappa):
    count_x, count_y = dims
    peers = count_x * count_y
    depth, size_x, size_y = pressure.shape
    levels, land = theta.shape
    slots = land // 32
    rows = land // 128
    flat = lambda value: value.reshape(rows, 128)
    grid = pltpu.VMEM((depth, size_x, size_y), F32)
    column = pltpu.VMEM((levels, rows, 128), F32)
    message = pltpu.VMEM((peers * 8, 128), F32)
    dma = pltpu.SemaphoreType.DMA
    vmem = pl.BlockSpec(memory_space=pltpu.VMEM)
    smem = pl.BlockSpec(memory_space=pltpu.SMEM)
    edge_x = pltpu.VMEM((2, 48, size_y), F32)
    edge2_x = pltpu.VMEM((2, 32, size_y), F32)
    edge_y = pltpu.VMEM((2, size_x, size_y), F32)
    rows_x = pltpu.VMEM((2, 16, size_y), F32)
    return pl.pallas_call(
        functools.partial(kernel, (count_x, count_y, slots)),
        out_shape=(
            jax.ShapeDtypeStruct(pressure.shape, F32),
            jax.ShapeDtypeStruct(pressure.shape, F32),
            jax.ShapeDtypeStruct(theta.shape, F32),
        ),
        in_specs=[smem] * 3 + [vmem] * 10,
        out_specs=(vmem, vmem, vmem),
        scratch_shapes=[
            pltpu.VMEM((slots, land), BF16),
            pltpu.VMEM((6 * peers, slots), F32),
            message, message, message, message,
            pltpu.VMEM((rows, 128), F32),
            grid, grid, grid, grid, grid, grid, grid, grid, grid,
            pltpu.VMEM((size_y, peers * slots), BF16),
            pltpu.VMEM((4 * size_x, size_y), F32),
            edge_x, edge_x, edge_y, edge_y, edge2_x, edge2_x, edge_y, edge_y,
            rows_x, edge_y, rows_x, edge_y,
            column, column, column,
            pltpu.VMEM((2 * size_x, 2 * size_y), BF16),
            dma((peers,)), dma((peers,)), dma((peers,)), dma((peers,)),
            dma((4,)), dma((4,)), dma((4,)), dma((4,)),
        ],
        compiler_params=pltpu.CompilerParams(
            collective_id=0, has_side_effects=True, vmem_limit_bytes=50 * 1024 * 1024
        ),
    )(
        ks_table, alpha_table, porosity_table, pressure, sat_old, soil_type,
        flat(rain), flat(evapo), flat(land_mask), flat(tile), flat(cell), theta, kappa,
    )


def solution(mesh):
    in_specs = (
        P(None, "gx", "gy"),
        P(None, "gx", "gy"),
        P(None, "gx", "gy"),
        P(),
        P(),
        P(),
        P(("gx", "gy")),
        P(("gx", "gy")),
        P(("gx", "gy")),
        P(("gx", "gy"), None),
        P(("gx", "gy")),
        P(None, ("gx", "gy")),
        P(None, ("gx", "gy")),
    )
    out_specs = (P(None, "gx", "gy"), P(None, "gx", "gy"), P(None, ("gx", "gy")))
    dims = (mesh.shape["gx"], mesh.shape["gy"])
    return jax.shard_map(
        functools.partial(local, dims), mesh=mesh, in_specs=in_specs, out_specs=out_specs, check_vma=False
    )
```

time: 327 us -> 48.1 us (0.15)
  local copies, waits for them, and re-layouts: 162 us -> 11.7 us
  other arithmetic: 120 us -> 0 us
  Pallas kernels: 0 us -> 35 us
  starting transfers between devices: 34.2 us -> 0 us
  waiting for transfers between devices: 7.59 us -> 0 us
    gather x19 -> x0, local copies, waits for them, and re-layouts: 73.9 us -> none  [the longest x2 32.8 us: local(): returned = returned.reshape(2, peers * slots)[:, slot]]
    scatter x2 -> x0, local copies, waits for them, and re-layouts: 53.5 us -> none  [the longest x1 30.5 us: local(): rank = jnp.zeros((land,), jnp.int32).at[order].set(rank_sorted)]
    scatter-add x1 -> x0, other arithmetic: 46.5 us -> none  [local(): jnp.zeros((2, size_x * size_y), jnp.float32).at[:, position]]
    pallas_call x0 -> x1, Pallas kernels: none -> 35 us  [local(): pl.pallas_call(functools.partial(kernel, (count_x, count_y, slots)), out_...]
    sub x4 -> x0, other arithmetic: 34.3 us -> none  [the longest x1 20.2 us: local(): rank_sorted = places - starts[sorted_target]]
    ppermute x8 -> x0, starting transfers between devices: 17.8 us -> none  [the longest x4 12.5 us: padded(): lax.ppermute(lax.slice_in_dim(block, block.shape[dim] - width, None, axis...]
    all_to_all x2 -> x0, starting transfers between devices: 16.3 us -> none  [the longest x1 8.92 us: local(): lax.all_to_all(answer.reshape(2, peers, slots), ('gx', 'gy'), split_axis=...]
    slice x11 -> x0, local copies, waits for them, and re-layouts: 14.8 us -> none  [the longest x1 6.93 us: local(): maps[0][None]]
  transfers between devices with their start and end apart: 10 -> 0, of which waited for: 4 -> 0; matrix products, arithmetic and copies ran while one was open for 22% -> 0% of each run, Pallas kernels for 0% -> 0%
where the time goes in v1:
time: 48.1 us; the launch traced here: 47.4 us
  Pallas kernels  35 us (73%)
  local copies, waits for them, and re-layouts  11.7 us (24%)
  between operations  0.68 us (1%)
    pallas_call x1, Pallas kernels, local(): pl.pallas_call(functools.partial(kernel, (count_x, count_y, slots)), out_...  35 us
    unnamed x29, local copies, waits for them, and re-layouts  11.7 us

profile of v1, /device:TPU:0, one launch (start us, length us, event | category | flops | bytes accessed | tf_op | source)
XLA Modules:
  0.0 47.4 jit_solution(11363982415120466194)
XLA Ops:
  0.6 0.0 copy-start.10
  0.6 0.0 copy-start.11
  0.7 0.0 copy-start.12
  0.7 0.6 %copy-done.10 = f32[13]{0:T(128)S(1)} copy-done((f32[13]{0:T(128)S(1)}, f32[13]{0:T(128)}, u32[]{:S(2)}) %copy-start.10) | copy-done | bytes 76
  1.3 0.0 copy-done.11
  1.3 0.0 copy-done.12
  1.3 0.0 copy-start
  1.3 1.0 %copy-done = f32[10,8192]{1,0:T(8,128)S(1)} copy-done((f32[10,8192]{1,0:T(8,128)S(1)}, f32[10,8192]{1,0:T(8,128)}, u32[]{:S(2)}) %copy-start) | copy-done | bytes 327704
  2.4 0.0 copy-start.1
  2.4 1.0 %copy-done.1 = f32[10,8192]{1,0:T(8,128)S(1)} copy-done((f32[10,8192]{1,0:T(8,128)S(1)}, f32[10,8192]{1,0:T(8,128)}, u32[]{:S(2)}) %copy-start.1) | copy-done | bytes 327704
  3.4 0.0 copy-start.2
  3.4 1.0 %copy-done.2 = f32[10,64,128]{2,1,0:T(8,128)S(1)} copy-done((f32[10,64,128]{2,1,0:T(8,128)S(1)}, f32[10,64,128]{2,1,0:T(8,128)}, u32[]{:S(2)}) %copy-start.2) | copy-done | bytes 327704
  4.4 0.0 copy-start.3
  4.4 1.0 %copy-done.3 = f32[10,64,128]{2,1,0:T(8,128)S(1)} copy-done((f32[10,64,128]{2,1,0:T(8,128)S(1)}, f32[10,64,128]{2,1,0:T(8,128)}, u32[]{:S(2)}) %copy-start.3) | copy-done | bytes 327704
  5.4 0.0 copy-start.4
  5.4 1.0 %copy-done.4 = s32[10,64,128]{2,1,0:T(8,128)S(1)} copy-done((s32[10,64,128]{2,1,0:T(8,128)S(1)}, s32[10,64,128]{2,1,0:T(8,128)}, u32[]{:S(2)}) %copy-start.4) | copy-done | bytes 327704
  6.3 0.0 copy-start.5
  6.3 0.8 %copy-done.5 = f32[8192]{0:T(1024)S(1)} copy-done((f32[8192]{0:T(1024)S(1)}, f32[8192]{0:T(1024)}, u32[]{:S(2)}) %copy-start.5) | copy-done | bytes 32792
  7.1 0.0 copy-start.6
  7.1 0.8 %copy-done.6 = f32[8192]{0:T(1024)S(1)} copy-done((f32[8192]{0:T(1024)S(1)}, f32[8192]{0:T(1024)}, u32[]{:S(2)}) %copy-start.6) | copy-done | bytes 32792
  7.8 0.0 copy-start.7
  7.8 0.8 %copy-done.7 = s32[8192]{0:T(1024)S(1)} copy-done((s32[8192]{0:T(1024)S(1)}, s32[8192]{0:T(1024)}, u32[]{:S(2)}) %copy-start.7) | copy-done | bytes 32792
  8.6 0.0 copy-start.8
  8.6 0.8 %copy-done.8 = s32[8192,1]{0,1:T(1,128)S(1)} copy-done((s32[8192,1]{0,1:T(1,128)S(1)}, s32[8192,1]{0,1:T(1,128)}, u32[]{:S(2)}) %copy-start.8) | copy-done | bytes 32792
  9.4 0.0 copy-start.9
  9.4 0.8 %copy-done.9 = s32[8192]{0:T(1024)S(1)} copy-done((s32[8192]{0:T(1024)S(1)}, s32[8192]{0:T(1024)}, u32[]{:S(2)}) %copy-start.9) | copy-done | bytes 32792
  10.1 35.0 %shard_map.148 = (f32[10,64,128]{2,1,0:T(8,128)S(1)}, f32[10,64,128]{2,1,0:T(8,128)S(1)}, f32[10,8192]{1,0:T(8,128)S(1)}) custom-call(f32[13]{0:T(128)S(1)} %copy-done.10, f32[13]{0:T(128)S(1)} %copy-done.11, f32[13]{0:T(128)S(1)} %copy-done.12, f32[10,64,128]{2,1,0:T(8,128)S(1)} %copy-done.2, f32[10,64,128]{2,1,0:T(8,128)S(1)} %copy-done.3, ...), custom_call_target="tpu_custom_call" | custom-call | tf_op jit(solution)/shard_map/pallas_call | solution.py:472
  45.2 0.7 %copy.19 = f32[10,64,128]{2,1,0:T(8,128)} copy(f32[10,64,128]{2,1,0:T(8,128)S(1)} %get-tuple-element.6) | data formatting | bytes 655360
  45.9 0.7 %copy.20 = f32[10,64,128]{2,1,0:T(8,128)} copy(f32[10,64,128]{2,1,0:T(8,128)S(1)} %get-tuple-element.7) | data formatting | bytes 655360
  46.6 0.8 %copy.21 = f32[10,8192]{1,0:T(8,128)} copy(f32[10,8192]{1,0:T(8,128)S(1)} %get-tuple-element.8) | data formatting | bytes 655360
Async XLA Ops:
  0.6 0.7 %copy-start.10 = (f32[13]{0:T(128)S(1)}, f32[13]{0:T(128)}, u32[]{:S(2)}) copy-start(f32[13]{0:T(128)} %ks_t.1) | copy-start | bytes 160
  0.6 0.7 %copy-start.11 = (f32[13]{0:T(128)S(1)}, f32[13]{0:T(128)}, u32[]{:S(2)}) copy-start(f32[13]{0:T(128)} %al_t.1) | copy-start | bytes 160
  0.7 0.7 %copy-start.12 = (f32[13]{0:T(128)S(1)}, f32[13]{0:T(128)}, u32[]{:S(2)}) copy-start(f32[13]{0:T(128)} %po_t.1) | copy-start | bytes 160
  1.3 1.0 %copy-start = (f32[10,8192]{1,0:T(8,128)S(1)}, f32[10,8192]{1,0:T(8,128)}, u32[]{:S(2)}) copy-start(f32[10,8192]{1,0:T(8,128)} %theta.1) | copy-start | bytes 983044
  2.4 1.0 %copy-start.1 = (f32[10,8192]{1,0:T(8,128)S(1)}, f32[10,8192]{1,0:T(8,128)}, u32[]{:S(2)}) copy-start(f32[10,8192]{1,0:T(8,128)} %kappa.1) | copy-start | bytes 983044
  3.4 1.0 %copy-start.2 = (f32[10,64,128]{2,1,0:T(8,128)S(1)}, f32[10,64,128]{2,1,0:T(8,128)}, u32[]{:S(2)}) copy-start(f32[10,64,128]{2,1,0:T(8,128)} %press.1) | copy-start | bytes 983044
  4.4 1.0 %copy-start.3 = (f32[10,64,128]{2,1,0:T(8,128)S(1)}, f32[10,64,128]{2,1,0:T(8,128)}, u32[]{:S(2)}) copy-start(f32[10,64,128]{2,1,0:T(8,128)} %sat_old.1) | copy-start | bytes 983044
  5.4 1.0 %copy-start.4 = (s32[10,64,128]{2,1,0:T(8,128)S(1)}, s32[10,64,128]{2,1,0:T(8,128)}, u32[]{:S(2)}) copy-start(s32[10,64,128]{2,1,0:T(8,128)} %soil.1) | copy-start | bytes 983044
  6.3 0.8 %copy-start.5 = (f32[8192]{0:T(1024)S(1)}, f32[8192]{0:T(1024)}, u32[]{:S(2)}) copy-start(f32[8192]{0:T(1024)} %param.19) | copy-start | bytes 98308
  7.1 0.8 %copy-start.6 = (f32[8192]{0:T(1024)S(1)}, f32[8192]{0:T(1024)}, u32[]{:S(2)}) copy-start(f32[8192]{0:T(1024)} %param.20) | copy-start | bytes 98308
  7.8 0.8 %copy-start.7 = (s32[8192]{0:T(1024)S(1)}, s32[8192]{0:T(1024)}, u32[]{:S(2)}) copy-start(s32[8192]{0:T(1024)} %param.21) | copy-start | bytes 98308
  8.6 0.8 %copy-start.8 = (s32[8192,1]{0,1:T(1,128)S(1)}, s32[8192,1]{0,1:T(1,128)}, u32[]{:S(2)}) copy-start(s32[8192,1]{0,1:T(1,128)} %param.22) | copy-start | bytes 98308
  9.4 0.8 %copy-start.9 = (s32[8192]{0:T(1024)S(1)}, s32[8192]{0:T(1024)}, u32[]{:S(2)}) copy-start(s32[8192]{0:T(1024)} %param.23) | copy-start | bytes 98308

commit v2 on v1

--- a/solution.py
+++ b/solution.py
@@ -36,21 +36,39 @@
     return jnp.where(product > 0, product / jnp.where(total > 0, total, 1.0), 0.0)
 
 
+def wide_row(row, count):
+    return jnp.concatenate([jnp.broadcast_to(row, (16, 128)).astype(BF16)] * (count // 16), axis=0)
+
+
+def iota16(count):
+    return lax.broadcasted_iota(jnp.int32, (count, 128), 0).astype(F32).astype(BF16)
+
+
 def iota(shape, dim):
     return lax.broadcasted_iota(jnp.int32, shape, dim)
 
 
 def kernel(
     dims,
-    ks_t, al_t, po_t,
-    press, sat_old, soil, rain, evapo, mask, tile, cell, theta, kappa,
-    p_out, r_out, t_out,
-    onehot, acc, send, recv, ans, ret, rank_s,
-    ks, al, phi, kr, gx, gy, gz, base, krn, oney, macc,
-    own_x, halo_x, own_y, halo_y, own2_x, halo2_x, own2_y, halo2_y, gbx, gby, fbx, fby,
-    th_s, ka_s, so_s, top_s,
-    send1, recv1, send2, recv2, hs1, hr1, hs2, hr2,
+    *refs,
 ):
+    given, refs = refs[:13], refs[13:]
+    (p_out, r_out, t_out), refs = refs[:3], refs[3:]
+    held, refs = refs[:13], refs[13:]
+    (ks_t, al_t, po_t, press, sat_old, soil, rain, evapo, mask, tile, cell, theta, kappa) = held
+    (
+        onehot, acc, send, recv, ans, ret,
+        ks, al, phi, kr, gx, gy, gz, base, krn, oney, macc,
+        own_x, halo_x, own_y, halo_y, own2_x, halo2_x, own2_y, halo2_y, gbx, gby, fbx, fby,
+        th_s, ka_s, so_s, top_s, found,
+        send1, recv1, send2, recv2, hs1, hr1, hs2, hr2, loaded,
+    ) = refs
+    loads = [
+        pltpu.make_async_copy(src, dst, loaded.at[n]) for n, (src, dst) in enumerate(zip(given, held))
+    ]
+    for n in (9, 8, 10, 6, 7, 5, 0, 1, 2, 3, 4, 11, 12):
+        loads[n].start()
+
     count_x, count_y, slots = dims
     peers = count_x * count_y
     depth, size_x, size_y = press.shape
@@ -78,6 +96,107 @@
 
     row_id = iota((size_x, size_y), 0)
     lane_id = iota((size_x, size_y), 1)
+
+    wide = iota((128, 256), 1)
+    tall = iota((128, 256), 0)
+    before = ((wide >= 128) | (tall < wide)).astype(F32).astype(BF16)
+    peer_id = iota((peers, 128), 0).astype(F32)
+    peer16 = iota16(peers)
+    slot16 = iota16(slots)
+    acc[...] = jnp.zeros_like(acc)
+    for n in (9, 8, 10, 6, 7):
+        loads[n].wait()
+
+    def dispatch(c, count):
+        at = pl.ds(pl.multiple_of(c * GROUP, GROUP), GROUP)
+        lanes = pl.ds(pl.multiple_of(c * GROUP * 128, 128), GROUP * 128)
+        named = tile[at, :]
+        live = mask[at, :].astype(F32)
+        where_to = cell[at, :].astype(F32)
+        cell_x = jnp.floor(where_to * (1.0 / size_y)) * size_y
+        values = (
+            *halves(live * rain[at, :]), *halves(live * evapo[at, :]), cell_x, where_to - cell_x
+        )
+        label = named.astype(F32)
+        hits = [label[i : i + 1, :] == peer_id for i in range(GROUP)]
+        hits16 = [wide_row(label[i : i + 1, :], peers) == peer16 for i in range(GROUP)]
+        one = jnp.ones((peers, 128), BF16)
+        sums = dot(
+            jnp.concatenate([jnp.where(h, one, jnp.zeros_like(one)) for h in hits16], axis=0), before, NN
+        )
+        ranks = []
+        for i in range(GROUP):
+            part = sums[i * peers : (i + 1) * peers]
+            ranks.append(
+                jnp.sum(jnp.where(hits[i], part[:, :128] + count, 0.0), axis=0, keepdims=True)
+            )
+            count = count + part[:, 128:]
+        one = jnp.ones((slots, 128), BF16)
+        chosen = jnp.concatenate(
+            [jnp.where(wide_row(r, slots) == slot16, one, jnp.zeros_like(one)) for r in ranks], axis=1
+        )
+        onehot[:, lanes] = chosen
+        nothing = jnp.zeros((peers, 128), BF16)
+        left = jnp.concatenate(
+            [
+                jnp.concatenate(
+                    [
+                        jnp.where(hits16[i], wide_row(v[i : i + 1, :], peers), nothing)
+                        for i in range(GROUP)
+                    ],
+                    axis=1,
+                )
+                for v in values
+            ],
+            axis=0,
+        )
+        acc[...] += dot(left, chosen, NT)
+        return count
+
+    lax.fori_loop(0, rows // GROUP, dispatch, jnp.zeros((peers, 128), F32), unroll=4)
+    for v in range(3):
+        full = acc[2 * v * peers : (2 * v + 1) * peers] + acc[(2 * v + 1) * peers : (2 * v + 2) * peers]
+        for h in range(parts):
+            send[pl.ds(v * parts + h, peers, stride=8), :] = full[:, h * 128 : (h + 1) * 128]
+
+    def block(ref, t):
+        return ref.at[pl.ds(pl.multiple_of(t * 8, 8), 8)]
+
+    def carry_over(src, dst, sems_s, sems_r, other, landing):
+        return pltpu.make_async_remote_copy(
+            src_ref=block(src, other), dst_ref=block(dst, landing),
+            send_sem=sems_s.at[other], recv_sem=sems_r.at[landing],
+            device_id=(other // count_y, lax.rem(other, count_y)), device_id_type=MESH,
+        )
+
+    def exchange(src, dst, sems_s, sems_r):
+        def step(i, carry):
+            other = lax.rem(me + i, peers)
+            carry_over(src, dst, sems_s, sems_r, other, me).start()
+            return carry
+
+        lax.fori_loop(1, peers, step, 0)
+        mine = pl.ds(pl.multiple_of(me * 8, 8), 8)
+        dst[mine, :] = src[mine, :]
+
+    def arrive(src, dst, sems_s, sems_r):
+        def step(i, carry):
+            other = lax.rem(me + i, peers)
+            carry_over(src, dst, sems_s, sems_r, other, other).wait_recv()
+            return carry
+
+        lax.fori_loop(1, peers, step, 0)
+
+    def sent(src, dst, sems_s, sems_r):
+        def step(i, carry):
+            other = lax.rem(me + i, peers)
+            carry_over(src, dst, sems_s, sems_r, other, me).wait_send()
+            return carry
+
+        lax.fori_loop(1, peers, step, 0)
+
+    pl.semaphore_wait(barrier, peers - 1)
+    exchange(send, recv, send1, recv1)
 
     def properties(z, carry):
         low, high = carry
@@ -104,12 +223,12 @@
             high = jnp.where(here, value[:, size_y - 1 :], high)
         return low, high
 
+    for n in (5, 0, 1, 2, 3):
+        loads[n].wait()
     blank = jnp.zeros((size_x, size_y), F32)
     low, high = lax.fori_loop(0, depth, properties, (blank, blank))
     own_y[0] = low
     own_y[1] = high
-
-    pl.semaphore_wait(barrier, peers - 1)
 
     def sides(src_x, dst_x, src_y, dst_y, sems_s, sems_r):
         plan = (
@@ -138,100 +257,17 @@
     for there, outward, _ in first_sides:
         pl.when(there)(outward.start)
 
-    wide = iota((128, 256), 1)
-    tall = iota((128, 256), 0)
-    before = ((wide >= 128) | (tall < wide)).astype(F32).astype(BF16)
-    peer_id = iota((peers, 128), 0)
-    slot_id = iota((slots, 128), 0).astype(F32)
-    acc[...] = jnp.zeros_like(acc)
-
-    def dispatch(c, count):
-        at = pl.ds(pl.multiple_of(c * GROUP, GROUP), GROUP)
-        lanes = pl.ds(pl.multiple_of(c * GROUP * 128, 128), GROUP * 128)
-        named = tile[at, :]
-        live = mask[at, :].astype(F32)
-        where_to = cell[at, :].astype(F32)
-        cell_x = jnp.floor(where_to * (1.0 / size_y)) * size_y
-        values = (
-            *halves(live * rain[at, :]), *halves(live * evapo[at, :]), cell_x, where_to - cell_x
-        )
-        hits = [named[i : i + 1, :] == peer_id for i in range(GROUP)]
-        ones = [jnp.where(h, 1.0, 0.0) for h in hits]
-        sums = dot(jnp.concatenate(ones, axis=0).astype(BF16), before, NN)
-        ranks = []
-        for i in range(GROUP):
-            part = sums[i * peers : (i + 1) * peers]
-            ranks.append(jnp.sum(ones[i] * (part[:, :128] + count), axis=0, keepdims=True))
-            count = count + part[:, 128:]
-        rank_s[at, :] = jnp.concatenate(ranks, axis=0)
-        chosen = jnp.concatenate(
-            [jnp.where(r == slot_id, 1.0, 0.0).astype(BF16) for r in ranks], axis=1
-        )
-        onehot[:, lanes] = chosen
-        left = jnp.concatenate(
-            [
-                jnp.concatenate(
-                    [jnp.where(hits[i], v[i : i + 1, :], 0.0) for i in range(GROUP)], axis=1
-                ).astype(BF16)
-                for v in values
-            ],
-            axis=0,
-        )
-        acc[...] += dot(left, chosen, NT)
-        return count
-
-    lax.fori_loop(0, rows // GROUP, dispatch, jnp.zeros((peers, 128), F32))
-    for v in range(3):
-        full = acc[2 * v * peers : (2 * v + 1) * peers] + acc[(2 * v + 1) * peers : (2 * v + 2) * peers]
-        for h in range(parts):
-            send[pl.ds(v * parts + h, peers, stride=8), :] = full[:, h * 128 : (h + 1) * 128]
-
-    def block(ref, t):
-        return ref.at[pl.ds(pl.multiple_of(t * 8, 8), 8)]
-
-    def carry_over(src, dst, sems_s, sems_r, other, landing):
-        return pltpu.make_async_remote_copy(
-            src_ref=block(src, other), dst_ref=block(dst, landing),
-            send_sem=sems_s.at[other], recv_sem=sems_r.at[landing],
-            device_id=(other // count_y, lax.rem(other, count_y)), device_id_type=MESH,
-        )
-
-    def exchange(src, dst, sems_s, sems_r):
-        def step(i, carry):
-            other = lax.rem(me + i, peers)
-            carry_over(src, dst, sems_s, sems_r, other, me).start()
-            return carry
-
-        lax.fori_loop(1, peers, step, 0)
-        mine = pl.ds(pl.multiple_of(me * 8, 8), 8)
-        dst[mine, :] = src[mine, :]
-
-    def arrive(src, dst, sems_s, sems_r):
-        def step(i, carry):
-            other = lax.rem(me + i, peers)
-            carry_over(src, dst, sems_s, sems_r, other, other).wait_recv()
-            return carry
-
-        lax.fori_loop(1, peers, step, 0)
-
-    def sent(src, dst, sems_s, sems_r):
-        def step(i, carry):
-            other = lax.rem(me + i, peers)
-            carry_over(src, dst, sems_s, sems_r, other, me).wait_send()
-            return carry
-
-        lax.fori_loop(1, peers, step, 0)
-
-    exchange(send, recv, send1, recv1)
-
     def spread(j, carry):
         lanes = pl.ds(pl.multiple_of(j * 128, 128), 128)
         for src, dst in ((theta, th_s), (kappa, ka_s)):
-            for k in range(levels):
-                dst[k, pl.ds(j, 1), :] = src[k : k + 1, lanes]
-        return carry
-
-    lax.fori_loop(0, rows, spread, 0)
+            for k in range(0, levels, 8):
+                n = min(8, levels - k)
+                dst[pl.ds(k * rows + j, n, stride=rows), :] = src[k : k + n, lanes]
+        return carry
+
+    for n in (11, 12, 4):
+        loads[n].wait()
+    lax.fori_loop(0, rows, spread, 0, unroll=8)
 
     def outflow(z, before_z, pr, rel):
         p = pr[z]
@@ -277,7 +313,8 @@
     arrive(send, recv, send1, recv1)
     macc[...] = jnp.zeros_like(macc)
     x_id = iota((size_x, 128), 0).astype(F32)
-    y_id = iota((size_y, 128), 0).astype(F32)
+    x16 = iota16(size_x)
+    y16 = iota16(size_y)
     srcs = GROUP // parts
 
     def gather_in(c, carry):
@@ -291,19 +328,25 @@
             at_y = got - at_x * size_y
             for h in range(parts):
                 n = 2 * parts + h
-                hit = at_x[n : n + 1, :] == x_id
-                right.append(jnp.where(at_y[n : n + 1, :] == y_id, 1.0, 0.0).astype(BF16))
+                hit = wide_row(at_x[n : n + 1, :], size_x) == x16
+                one = jnp.ones((size_y, 128), BF16)
+                nothing = jnp.zeros((size_x, 128), BF16)
+                right.append(
+                    jnp.where(wide_row(at_y[n : n + 1, :], size_y) == y16, one, jnp.zeros_like(one))
+                )
                 for v in range(2):
                     m = v * parts + h
-                    left[2 * v].append(jnp.where(hit, high_v[m : m + 1, :], 0.0).astype(BF16))
-                    left[2 * v + 1].append(jnp.where(hit, low_v[m : m + 1, :], 0.0).astype(BF16))
+                    high_row = wide_row(high_v[m : m + 1, :], size_x)
+                    low_row = wide_row(low_v[m : m + 1, :], size_x)
+                    left[2 * v].append(jnp.where(hit, high_row, nothing))
+                    left[2 * v + 1].append(jnp.where(hit, low_row, nothing))
         right = jnp.concatenate(right, axis=1)
         oney[:, lanes] = right
         left = jnp.concatenate([jnp.concatenate(l, axis=1) for l in left], axis=0)
         macc[...] += dot(left, right, NT)
         return carry
 
-    lax.fori_loop(0, peers * parts // GROUP, gather_in, 0)
+    lax.fori_loop(0, peers * parts // GROUP, gather_in, 0, unroll=4)
     rain_map = macc[0:size_x] + macc[size_x : 2 * size_x]
     et_map = macc[2 * size_x : 3 * size_x] + macc[3 * size_x : 4 * size_x]
 
@@ -358,7 +401,7 @@
             ans[at, :] = jnp.concatenate(out, axis=0)
         return carry
 
-    lax.fori_loop(0, peers * parts // GROUP, answer, 0)
+    lax.fori_loop(0, peers * parts // GROUP, answer, 0, unroll=4)
     exchange(ans, ret, send2, recv2)
 
     for there, _, inward in second_sides:
@@ -387,37 +430,41 @@
         tops.extend(halves(value))
     tops = jnp.concatenate(tops, axis=0).astype(BF16)
 
-    def solve(c, carry):
+    def pick(c, carry):
         at = pl.ds(pl.multiple_of(c * GROUP, GROUP), GROUP)
         lanes = pl.ds(pl.multiple_of(c * GROUP * 128, 128), GROUP * 128)
-        named = tile[at, :]
+        label = tile[at, :].astype(F32)
         picked = dot(tops, onehot[:, lanes], NN)
-        both = []
         for v in range(2):
             value = picked[2 * v * peers : (2 * v + 1) * peers]
             value = value + picked[(2 * v + 1) * peers : (2 * v + 2) * peers]
-            both.append(
-                jnp.concatenate(
-                    [
-                        jnp.sum(
-                            jnp.where(
-                                named[i : i + 1, :] == peer_id, value[:, i * 128 : (i + 1) * 128], 0.0
-                            ),
-                            axis=0, keepdims=True,
-                        )
-                        for i in range(GROUP)
-                    ],
-                    axis=0,
-                )
+            found[v, at, :] = jnp.concatenate(
+                [
+                    jnp.sum(
+                        jnp.where(label[i : i + 1, :] == peer_id, value[:, i * 128 : (i + 1) * 128], 0.0),
+                        axis=0, keepdims=True,
+                    )
+                    for i in range(GROUP)
+                ],
+                axis=0,
             )
-        p_top, s_top = both
+        return carry
+
+    lax.fori_loop(0, rows // GROUP, pick, 0, unroll=4)
+
+    many = 4 * GROUP
+
+    def solve(c, carry):
+        at = pl.ds(pl.multiple_of(c * many, many), many)
+        ats = [pl.ds(pl.multiple_of(k * rows + c * many, GROUP), many) for k in range(levels)]
+        p_top, s_top = found[0, at, :], found[1, at, :]
         active = mask[at, :] == 1
-        coeff = [ka_s[k, at, :] * (0.5 + s_top) for k in range(levels)]
+        coeff = [ka_s[ats[k], :] * (0.5 + s_top) for k in range(levels)]
         coeff.append(jnp.zeros_like(p_top))
         upper, value = [], []
         for k in range(levels):
             diag = 1.0 + coeff[k] + coeff[k + 1]
-            right = th_s[k, at, :]
+            right = th_s[ats[k], :]
             if k == 0:
                 right = right + coeff[0] * p_top
             else:
@@ -427,27 +474,37 @@
             upper.append(coeff[k + 1] * inverse)
             value.append(right * inverse)
         result = value[-1]
-        so_s[levels - 1, at, :] = jnp.where(active, result, th_s[levels - 1, at, :])
+        so_s[ats[levels - 1], :] = jnp.where(active, result, th_s[ats[levels - 1], :])
         for k in range(levels - 2, -1, -1):
             result = value[k] + upper[k] * result
-            so_s[k, at, :] = jnp.where(active, result, th_s[k, at, :])
-        return carry
-
-    lax.fori_loop(0, rows // GROUP, solve, 0)
+            so_s[ats[k], :] = jnp.where(active, result, th_s[ats[k], :])
+        return carry
+
+    lax.fori_loop(0, rows // many, solve, 0)
 
     def collect(j, carry):
         lanes = pl.ds(pl.multiple_of(j * 128, 128), 128)
-        for k in range(levels):
-            t_out[k : k + 1, lanes] = so_s[k, pl.ds(j, 1), :]
-        return carry
-
-    lax.fori_loop(0, rows, collect, 0)
+        for k in range(0, levels, 8):
+            n = min(8, levels - k)
+            t_out[k : k + n, lanes] = so_s[pl.ds(k * rows + j, n, stride=rows), :]
+        return carry
+
+    lax.fori_loop(0, rows, collect, 0, unroll=8)
 
     sent(send, recv, send1, recv1)
     sent(ans, ret, send2, recv2)
     for made in (first_sides, second_sides):
         for there, outward, _ in made:
             pl.when(there)(outward.wait_send)
+
+
+def write_out(*refs):
+    done = refs[6]
+    copies = [pltpu.make_async_copy(refs[n], refs[n + 3], done.at[n]) for n in range(3)]
+    for copy in copies:
+        copy.start()
+    for copy in copies:
+        copy.wait()
 
 
 def local(dims, pressure, sat_old, soil_type, ks_table, alpha_table, porosity_table,
@@ -460,29 +517,35 @@
     rows = land // 128
     flat = lambda value: value.reshape(rows, 128)
     grid = pltpu.VMEM((depth, size_x, size_y), F32)
-    column = pltpu.VMEM((levels, rows, 128), F32)
+    column = pltpu.VMEM((levels * rows, 128), F32)
     message = pltpu.VMEM((peers * 8, 128), F32)
     dma = pltpu.SemaphoreType.DMA
     vmem = pl.BlockSpec(memory_space=pltpu.VMEM)
-    smem = pl.BlockSpec(memory_space=pltpu.SMEM)
     edge_x = pltpu.VMEM((2, 48, size_y), F32)
     edge2_x = pltpu.VMEM((2, 32, size_y), F32)
     edge_y = pltpu.VMEM((2, size_x, size_y), F32)
     rows_x = pltpu.VMEM((2, 16, size_y), F32)
-    return pl.pallas_call(
+    args = (
+        ks_table, alpha_table, porosity_table, pressure, sat_old, soil_type,
+        flat(rain), flat(evapo), flat(land_mask), flat(tile), flat(cell), theta, kappa,
+    )
+    held = [pltpu.SMEM(a.shape, a.dtype) for a in args[:3]]
+    held += [pltpu.VMEM(a.shape, a.dtype) for a in args[3:]]
+    hbm = pl.BlockSpec(memory_space=pltpu.HBM)
+    outs = pl.pallas_call(
         functools.partial(kernel, (count_x, count_y, slots)),
         out_shape=(
-            jax.ShapeDtypeStruct(pressure.shape, F32),
-            jax.ShapeDtypeStruct(pressure.shape, F32),
-            jax.ShapeDtypeStruct(theta.shape, F32),
+            pltpu.VMEM(pressure.shape, F32),
+            pltpu.VMEM(pressure.shape, F32),
+            pltpu.VMEM(theta.shape, F32),
         ),
-        in_specs=[smem] * 3 + [vmem] * 10,
+        in_specs=[hbm] * len(args),
         out_specs=(vmem, vmem, vmem),
         scratch_shapes=[
+            *held,
             pltpu.VMEM((slots, land), BF16),
             pltpu.VMEM((6 * peers, slots), F32),
             message, message, message, message,
-            pltpu.VMEM((rows, 128), F32),
             grid, grid, grid, grid, grid, grid, grid, grid, grid,
             pltpu.VMEM((size_y, peers * slots), BF16),
             pltpu.VMEM((4 * size_x, size_y), F32),
@@ -490,16 +553,22 @@
             rows_x, edge_y, rows_x, edge_y,
             column, column, column,
             pltpu.VMEM((2 * size_x, 2 * size_y), BF16),
+            pltpu.VMEM((2, rows, 128), F32),
             dma((peers,)), dma((peers,)), dma((peers,)), dma((peers,)),
-            dma((4,)), dma((4,)), dma((4,)), dma((4,)),
+            dma((4,)), dma((4,)), dma((4,)), dma((4,)), dma((len(args),)),
         ],
         compiler_params=pltpu.CompilerParams(
-            collective_id=0, has_side_effects=True, vmem_limit_bytes=50 * 1024 * 1024
+            collective_id=0, has_side_effects=True, vmem_limit_bytes=60 * 1024 * 1024
         ),
-    )(
-        ks_table, alpha_table, porosity_table, pressure, sat_old, soil_type,
-        flat(rain), flat(evapo), flat(land_mask), flat(tile), flat(cell), theta, kappa,
-    )
+    )(*args)
+    return pl.pallas_call(
+        write_out,
+        out_shape=tuple(jax.ShapeDtypeStruct(o.shape, F32) for o in outs),
+        in_specs=[vmem] * 3,
+        out_specs=(hbm, hbm, hbm),
+        scratch_shapes=[dma((3,))],
+        compiler_params=pltpu.CompilerParams(vmem_limit_bytes=8 * 1024 * 1024),
+    )(*outs)
 
 
 def solution(mesh):

time: 48.1 us -> 28.7 us (0.60); the launches traced: 47.4 us -> 28.5 us
  local copies, waits for them, and re-layouts: 11.7 us -> 0 us
  Pallas kernels: 35 us -> 27.9 us
    unnamed x29 -> x0, local copies, waits for them, and re-layouts: 11.7 us -> none
    pallas_call x1, Pallas kernels: 35 us -> 26.9 us  [local(): pl.pallas_call(functools.partial(kernel, (count_x, count_y, slots)), out_...]
    pallas_call x0 -> x1, Pallas kernels: none -> 1.04 us  [local(): pl.pallas_call(write_out, out_shape=tuple((jax.ShapeDtypeStruct(o.shape,...]
where the time goes in v2:
time: 28.7 us; the launch traced here: 28.5 us
  Pallas kernels  27.9 us (97%)
  between operations  0.64 us (2%)
    pallas_call x1, Pallas kernels, local(): pl.pallas_call(functools.partial(kernel, (count_x, count_y, slots)), out_...  26.9 us
    pallas_call x1, Pallas kernels, local(): pl.pallas_call(write_out, out_shape=tuple((jax.ShapeDtypeStruct(o.shape,...  1.04 us

profile of v2, /device:TPU:0, one launch (start us, length us, event | category | flops | bytes accessed | tf_op | source)
XLA Modules:
  0.0 28.5 jit_solution(8032719916065769807)
XLA Ops:
  0.6 26.9 %shard_map.148 = (f32[10,64,128]{2,1,0:T(8,128)S(1)}, f32[10,64,128]{2,1,0:T(8,128)S(1)}, f32[10,8192]{1,0:T(8,128)S(1)}) custom-call(f32[13]{0:T(128)} %refs_0_.1, f32[13]{0:T(128)} %refs_1_.1, f32[13]{0:T(128)} %refs_2_.1, f32[10,64,128]{2,1,0:T(8,128)} %refs_3_.1, f32[10,64,128]{2,1,0:T(8,128)} %refs_4_.1, s32[10,64,128]{2,1,0:T(8,128)} %refs_5_.1, ...), custom_call_target="tpu_custom_call" | custom-call | tf_op jit(solution)/shard_map/pallas_call | solution.py:535
  27.5 1.0 %shard_map.149 = (f32[10,64,128]{2,1,0:T(8,128)}, f32[10,64,128]{2,1,0:T(8,128)}, f32[10,8192]{1,0:T(8,128)}) custom-call(f32[10,64,128]{2,1,0:T(8,128)S(1)} %get-tuple-element.6.refs_0_, f32[10,64,128]{2,1,0:T(8,128)S(1)} %get-tuple-element.7.refs_1_, f32[10,8192]{1,0:T(8,128)S(1)} %get-tuple-element.8.refs_2_), custom_call_target="tpu_custom_call" | custom-call | tf_op jit(solution)/shard_map/pallas_call | solution.py:564

commit v3 on v2

--- a/solution.py
+++ b/solution.py
@@ -165,7 +165,7 @@
     def carry_over(src, dst, sems_s, sems_r, other, landing):
         return pltpu.make_async_remote_copy(
             src_ref=block(src, other), dst_ref=block(dst, landing),
-            send_sem=sems_s.at[other], recv_sem=sems_r.at[landing],
+            send_sem=sems_s, recv_sem=sems_r,
             device_id=(other // count_y, lax.rem(other, count_y)), device_id_type=MESH,
         )
 
@@ -179,21 +179,19 @@
         mine = pl.ds(pl.multiple_of(me * 8, 8), 8)
         dst[mine, :] = src[mine, :]
 
-    def arrive(src, dst, sems_s, sems_r):
-        def step(i, carry):
-            other = lax.rem(me + i, peers)
-            carry_over(src, dst, sems_s, sems_r, other, other).wait_recv()
-            return carry
-
-        lax.fori_loop(1, peers, step, 0)
-
-    def sent(src, dst, sems_s, sems_r):
-        def step(i, carry):
-            other = lax.rem(me + i, peers)
-            carry_over(src, dst, sems_s, sems_r, other, me).wait_send()
-            return carry
-
-        lax.fori_loop(1, peers, step, 0)
+    def everything(src, dst, sems_s, sems_r):
+        most = pl.ds(0, (peers - 1) * 8)
+        other = lax.rem(me + 1, peers)
+        return pltpu.make_async_remote_copy(
+            src_ref=src.at[most], dst_ref=dst.at[most], send_sem=sems_s, recv_sem=sems_r,
+            device_id=(other // count_y, lax.rem(other, count_y)), device_id_type=MESH,
+        )
+
+    def arrive(*way):
+        everything(*way).wait_recv()
+
+    def sent(*way):
+        everything(*way).wait_send()
 
     pl.semaphore_wait(barrier, peers - 1)
     exchange(send, recv, send1, recv1)
@@ -381,11 +379,13 @@
     top_s[...] = jnp.concatenate(fields, axis=0).astype(BF16)
 
     def answer(c, carry):
-        lanes = pl.ds(pl.multiple_of(c * GROUP * 128, 128), GROUP * 128)
-        right = oney[:, lanes]
+        others = [lax.rem(me + c * srcs + i + 1, peers) for i in range(srcs)]
+        right = jnp.concatenate(
+            [oney[:, pl.ds(pl.multiple_of(o * slots, slots), slots)] for o in others], axis=1
+        )
         picked = dot(top_s[...], jnp.concatenate([right, right], axis=0), NN)
-        for i in range(srcs):
-            at = pl.ds(pl.multiple_of((c * srcs + i) * 8, 8), 8)
+        for i, other in enumerate(others):
+            at = pl.ds(pl.multiple_of(other * 8, 8), 8)
             at_x = jnp.floor(recv[at, :] * (1.0 / size_y))
             out = [None] * (2 * parts)
             for h in range(parts):
@@ -399,10 +399,21 @@
                     )
             out.append(jnp.zeros((8 - 2 * parts, 128), F32))
             ans[at, :] = jnp.concatenate(out, axis=0)
-        return carry
-
-    lax.fori_loop(0, peers * parts // GROUP, answer, 0, unroll=4)
-    exchange(ans, ret, send2, recv2)
+        for other in others[: srcs - 1]:
+            carry_over(ans, ret, send2, recv2, other, me).start()
+        return carry
+
+    turns = peers // srcs
+    lax.fori_loop(0, turns, answer, 0, unroll=4)
+
+    def rest(c, carry):
+        other = lax.rem(me + (c + 1) * srcs, peers)
+        carry_over(ans, ret, send2, recv2, other, me).start()
+        return carry
+
+    lax.fori_loop(0, turns - 1, rest, 0)
+    mine = pl.ds(pl.multiple_of(me * 8, 8), 8)
+    ret[mine, :] = ans[mine, :]
 
     for there, _, inward in second_sides:
         pl.when(there)(inward.wait_recv)
@@ -554,7 +565,7 @@
             column, column, column,
             pltpu.VMEM((2 * size_x, 2 * size_y), BF16),
             pltpu.VMEM((2, rows, 128), F32),
-            dma((peers,)), dma((peers,)), dma((peers,)), dma((peers,)),
+            dma, dma, dma, dma,
             dma((4,)), dma((4,)), dma((4,)), dma((4,)), dma((len(args),)),
         ],
         compiler_params=pltpu.CompilerParams(

time: 28.7 us -> 26.3 us (0.916)
  Pallas kernels: 27.9 us -> 25.5 us
    pallas_call x1, Pallas kernels: 26.9 us -> 24.5 us  [local(): pl.pallas_call(functools.partial(kernel, (count_x, count_y, slots)), out_...]
where the time goes in v3:
time: 26.3 us; the launch traced here: 26.1 us
  Pallas kernels  25.5 us (97%)
  between operations  0.64 us (2%)
    pallas_call x1, Pallas kernels, local(): pl.pallas_call(functools.partial(kernel, (count_x, count_y, slots)), out_...  24.5 us
    pallas_call x1, Pallas kernels, local(): pl.pallas_call(write_out, out_shape=tuple((jax.ShapeDtypeStruct(o.shape,...  1.04 us

profile of v3, /device:TPU:0, one launch (start us, length us, event | category | flops | bytes accessed | tf_op | source)
XLA Modules:
  0.0 26.1 jit_solution(10496328519943050410)
XLA Ops:
  0.6 24.5 %shard_map.148 = (f32[10,64,128]{2,1,0:T(8,128)S(1)}, f32[10,64,128]{2,1,0:T(8,128)S(1)}, f32[10,8192]{1,0:T(8,128)S(1)}) custom-call(f32[13]{0:T(128)} %refs_0_.1, f32[13]{0:T(128)} %refs_1_.1, f32[13]{0:T(128)} %refs_2_.1, f32[10,64,128]{2,1,0:T(8,128)} %refs_3_.1, f32[10,64,128]{2,1,0:T(8,128)} %refs_4_.1, s32[10,64,128]{2,1,0:T(8,128)} %refs_5_.1, ...), custom_call_target="tpu_custom_call" | custom-call | tf_op jit(solution)/shard_map/pallas_call | solution.py:546
  25.1 1.0 %shard_map.149 = (f32[10,64,128]{2,1,0:T(8,128)}, f32[10,64,128]{2,1,0:T(8,128)}, f32[10,8192]{1,0:T(8,128)}) custom-call(f32[10,64,128]{2,1,0:T(8,128)S(1)} %get-tuple-element.6.refs_0_, f32[10,64,128]{2,1,0:T(8,128)S(1)} %get-tuple-element.7.refs_1_, f32[10,8192]{1,0:T(8,128)S(1)} %get-tuple-element.8.refs_2_), custom_call_target="tpu_custom_call" | custom-call | tf_op jit(solution)/shard_map/pallas_call | solution.py:575
